TPU v7x, 256 devices: a whole 4x4x8 slice. The times are simulated.
256 devices in a mesh: layer: 4 (over z_hi, core), query: 4 (over z_lo), doc: 16 (over y, x).
Axes of the slice: x: 4, y: 4, z: 8 (z_hi: 2, z_lo: 4; z = z_hi * 4 + z_lo), core: 2. Of those that a mesh axis runs over, the one named last changes fastest.
Arguments:
- query_out: bfloat16 [256, 11008], P(None, 'doc'), may hold values from -0.21875 to 0.21875
- query_in: bfloat16 [256, 4096], P(None, 'doc'), may hold values from -0.21875 to 0.21875
- basis_out: bfloat16 [11008, 11008], P('doc', 'layer'), may hold values from -0.0546875 to 0.0546875
- basis_in: bfloat16 [4096, 4096], P('doc', 'query'), may hold values from -0.09375 to 0.09375
- eigenvalues: bfloat16 [11008, 4096], P('layer', ('query', 'doc')), may hold values from 0.049804688 to 5
- doc_out: bfloat16 [64, 64, 11008], P('doc', None, 'layer'), may hold values from -0.21875 to 0.21875
- doc_in: bfloat16 [64, 64, 4096], P('doc', None, 'query'), may hold values from -0.21875 to 0.21875
- pair_list: int32 [64, 2], P('doc'), may hold values from 0 to 3, as said below
- pair_count: int32 [16], P('doc'), may hold values from 1 to 4, as said below
Outputs:
- scores: float32 [64, 4], P('doc')
Inputs may be any that keep to these rules, and one draw needn't show every extreme that they name: `pair_list`: A row of a doc device's list is live when its position is below that device's count; column 0 is a query block below 4, column 1 one of the device's own 4 blocks; rows past the count hold ids in the same ranges and are ignored. `pair_count`: one doc device holds exactly 4 live slots in every draw.
All inputs are finite; a program needn't handle non-finite values.
Results may differ from a plain program's by a relative error of at most 0.0063.
Values may be sent and summed in bfloat16 or wider, within the bound.
No kernel may reach another device: no remote copies, remote signals or barrier semaphores. Data moves between devices by JAX's collectives and lax.ppermute only.
A program may use at most 128 MiB of HBM per device.

v0:
```python
import jax
import jax.numpy as jnp
from jax import lax
from jax.experimental import pallas as pl
from jax.experimental.pallas import tpu as pltpu
from jax.sharding import PartitionSpec as P

FACTOR_RANK = 32
QUERY_BLOCK = 2
DOC_BLOCK = 2
TILE = 256
LANES = 128
SIDE = 4
SCALE = 4096.0

damping = 0.1

ODD, CORE, ROW, COLUMN = range(4)
STEPS = (0, SIDE - 1, 1, 2)


def arrange_kernel(here, low_ref, high_ref, rows_ref, columns, *, swap):
    low = low_ref[...].astype(jnp.float32).T
    high = high_ref[...].astype(jnp.float32).T
    half = low.shape[1]
    if swap:
        keep = here[ODD] == here[CORE]
        low, high = jnp.where(keep, low, high), jnp.where(keep, high, low)
    columns[:, :half] = low
    columns[:, half:] = high
    size = columns.shape[0] // (SIDE * SIDE)
    first = here[CORE] == 0
    for outer in range(SIDE):
        for inner in range(SIDE):
            row = lax.rem(here[ROW] + jnp.where(first, STEPS[outer], STEPS[inner]), SIDE)
            column = lax.rem(here[COLUMN] + jnp.where(first, STEPS[inner], STEPS[outer]), SIDE)
            source = pl.multiple_of((row * SIDE + column) * size, size)
            place = (outer * SIDE + inner) * size
            rows_ref[place:place + size, :] = columns[pl.ds(source, size), :].astype(jnp.bfloat16)


def arrange(here, low, high, low_map, high_map, model, swap):
    half = 2 * FACTOR_RANK * QUERY_BLOCK
    return pl.pallas_call(
        lambda *refs: arrange_kernel(*refs, swap=swap),
        out_shape=jax.ShapeDtypeStruct((model, 2 * half), jnp.bfloat16),
        grid_spec=pltpu.PrefetchScalarGridSpec(
            num_scalar_prefetch=1,
            grid=(1,),
            in_specs=[pl.BlockSpec((half, model), low_map), pl.BlockSpec((half, model), high_map)],
            out_specs=pl.BlockSpec((model, 2 * half), lambda i, here: (0, 0)),
            scratch_shapes=[pltpu.VMEM((model, 2 * half), jnp.float32)],
        ),
        compiler_params=pltpu.CompilerParams(vmem_limit_bytes=32 * 2**20),
        cost_estimate=pl.CostEstimate(flops=0, bytes_accessed=4 * model * half * 2, transcendentals=0),
    )(here, low, high)


def score_kernel(pairs, count, here, *refs, spread, last):
    own_ref, refs = refs[0], refs[1:]
    if last:
        far_ref, earlier_ref, refs = refs[0], refs[1], refs[2:]
    query_ref, doc_ref, doc_rows_ref = refs[:3]
    eigen_refs = refs[3:3 + len(spread)]
    result_ref, eigen, weights, scaled, total, sems = refs[3 + len(spread):9 + len(spread)]
    step = pl.program_id(0)
    padded = doc_rows_ref.shape[1]
    first = own_ref.shape[1] - padded
    band = weights.shape[0]
    bands = max(spread) + 1
    slots = pairs.shape[1]
    blocks = total.shape[0] // QUERY_BLOCK
    if last:
        rows, first, half = refs[-1], 0, own_ref.shape[0]
        begin_place = jnp.where(step < bands - 1, blocks // 2, 0)
        end_place = blocks
    else:
        rows, begin_place, end_place = own_ref, 0, blocks // 2

    def fetch(which, start):
        offset = 0
        for number, place in enumerate(spread):
            if place == which:
                size = eigen_refs[number].shape[0]
                copy = pltpu.make_async_copy(
                    eigen_refs[number], eigen.at[which % 2, pl.ds(offset, size)], sems.at[number]
                )
                copy.start() if start else copy.wait()
                offset += size

    @pl.when(step == 0)
    def _():
        fetch(0, True)
        if last:
            total[...] = earlier_ref[...]
            rows[:half] = own_ref[:, own_ref.shape[1] - padded:]
            rows[half:] = far_ref[...]
        else:
            total[...] = jnp.zeros_like(total)

    for which in range(bands):
        @pl.when(step == which)
        def _():
            fetch(which, False)
            if which + 1 < bands:
                fetch(which + 1, True)

    shifted = eigen[lax.rem(step, 2)].astype(jnp.float32) + damping
    guess = pl.reciprocal(shifted, approx=True)
    weights[...] = guess * (2.0 - shifted * guess)
    query_side = query_ref[...]
    doc_side = doc_ref[...].astype(jnp.float32)
    lane = lax.broadcasted_iota(jnp.int32, query_side.shape, 1) // FACTOR_RANK
    empty = jnp.zeros_like(query_side)

    def score(places):
        left = jnp.concatenate(
            [
                jnp.where(lane == place * QUERY_BLOCK + q, query_side, empty)
                for place in places for q in range(QUERY_BLOCK)
            ],
            axis=0,
        )
        parts = len(places) * QUERY_BLOCK
        for begin in range(0, padded, TILE):
            end = begin + TILE
            product = jnp.dot(
                left, rows[:, first + begin:first + end], preferred_element_type=jnp.float32
            )
            for q in range(parts):
                part = slice(q * band, (q + 1) * band)
                scaled[part, begin:end] = (product[part] * weights[:, begin:end]).astype(jnp.bfloat16)
        mixed = lax.dot_general(
            scaled[:parts * band], doc_rows_ref[...], (((1,), (1,)), ((), ())),
            preferred_element_type=jnp.float32,
        )
        for q in range(parts):
            part = mixed[q * band:(q + 1) * band] * doc_side
            block = lax.rem(places[q // QUERY_BLOCK] + here[ODD] * (blocks // 2), blocks)
            row = block * QUERY_BLOCK + q % QUERY_BLOCK
            total[pl.ds(row, 1), :] += jnp.sum(part, axis=0, keepdims=True)

    def wanted(place):
        block = lax.rem(place + here[ODD] * (blocks // 2), blocks)
        found = jnp.bool_(False)
        for slot in range(slots):
            found = found | ((pairs[0, slot] == block) & (count[0] > slot))
        return found

    @pl.loop(begin_place // 2, end_place // 2)
    def _(pair):
        lower, upper = wanted(2 * pair), wanted(2 * pair + 1)

        @pl.when(lower & upper)
        def _():
            score((2 * pair, 2 * pair + 1))

        @pl.when(lower != upper)
        def _():
            score((2 * pair + jnp.where(upper, 1, 0),))

    @pl.when(step == bands - 1)
    def _():
        if not last:
            result_ref[...] = total[...]
            return
        sums = total[...]
        row = lax.broadcasted_iota(jnp.int32, sums.shape, 0)
        doc = lax.broadcasted_iota(jnp.int32, sums.shape, 1) // FACTOR_RANK
        query = jnp.full(sums.shape, -1, jnp.int32)
        block = jnp.full(sums.shape, -1, jnp.int32)
        for number in range(sums.shape[0] // QUERY_BLOCK):
            inside = (row // QUERY_BLOCK == number) & (count[0] > number)
            query = jnp.where(inside, pairs[0, number] * QUERY_BLOCK + row % QUERY_BLOCK, query)
            block = jnp.where(inside, pairs[1, number], block)
        picked = jnp.zeros_like(sums)
        for number in range(sums.shape[0]):
            picked = jnp.where(query == number, sums[number:number + 1], picked)
        column = lax.broadcasted_iota(jnp.int32, result_ref.shape, 1)
        result = jnp.zeros(result_ref.shape, jnp.float32)
        for d in range(DOC_BLOCK):
            value = jnp.sum(
                jnp.where(doc == block * DOC_BLOCK + d, picked, 0.0), axis=1, keepdims=True
            )
            result = jnp.where(column == d, value, result)
        result_ref[...] = result


def slot_scores(scalars, own, query_side, doc_side, doc_rows, eigen, spread, rest=()):
    model, queries = query_side.shape
    docs = doc_side.shape[1]
    last = bool(rest)
    padded = doc_rows.shape[1]
    bands = max(spread) + 1
    band = sum(rows.shape[0] for rows, place in zip(eigen, spread) if place == 0)
    lanes = queries if last else queries // 2
    out_rows = queries // FACTOR_RANK
    whole = lambda array: pl.BlockSpec(array.shape, lambda j, *_: (0, 0))
    in_specs = [whole(array) for array in (own, *rest)] + [
        pl.BlockSpec((band, lanes), lambda j, *_: (j, 0)),
        pl.BlockSpec((band, docs), lambda j, *_: (j, 0)),
        whole(doc_rows),
    ] + [pl.BlockSpec(memory_space=pl.ANY)] * len(eigen)
    shape = (out_rows, LANES if last else docs)
    scratch = [
        pltpu.VMEM((2, band, padded), jnp.bfloat16),
        pltpu.VMEM((band, padded), jnp.float32),
        pltpu.VMEM((2 * QUERY_BLOCK * band, padded), jnp.bfloat16),
        pltpu.VMEM((out_rows, docs), jnp.float32),
        pltpu.SemaphoreType.DMA((len(eigen),)),
    ]
    if last:
        scratch.append(pltpu.VMEM((queries, padded), jnp.bfloat16))
    return pl.pallas_call(
        lambda *refs: score_kernel(*refs, spread=spread, last=last),
        out_shape=jax.ShapeDtypeStruct(shape, jnp.float32),
        grid_spec=pltpu.PrefetchScalarGridSpec(
            num_scalar_prefetch=len(scalars),
            grid=(bands,),
            in_specs=in_specs,
            out_specs=pl.BlockSpec(shape, lambda j, *_: (0, 0)),
            scratch_shapes=scratch,
        ),
        compiler_params=pltpu.CompilerParams(
            dimension_semantics=("arbitrary",), vmem_limit_bytes=40 * 2**20
        ),
        cost_estimate=pl.CostEstimate(
            flops=2 * 2 * 2 * QUERY_BLOCK * bands * band * queries * padded,
            bytes_accessed=4 * bands * band * padded + 4 * 2**20, transcendentals=0,
        ),
    )(*scalars, own, *rest, query_side, doc_side, doc_rows, *eigen)


def local(
    query_out, query_in, basis_out, basis_in, eigenvalues, doc_out, doc_in, pair_list, pair_count
):
    layer, query, doc = (lax.axis_index(axis) for axis in ("layer", "query", "doc"))
    parts = lax.axis_size("doc")
    core = layer % 2
    odd = query % 2
    y, x = doc // SIDE, doc % SIDE
    model = doc_in.shape[2]

    def shift(array, by, first):
        pairs = []
        for source in range(lax.axis_size("layer") * parts):
            at, (row, column) = source // parts, divmod(source % parts, SIDE)
            if (at % 2 == 0) == first:
                column = (column + by) % SIDE
            else:
                row = (row + by) % SIDE
            pairs.append((source, at * parts + row * SIDE + column))
        return lax.ppermute(array, ("layer", "doc"), pairs)

    here = jnp.stack([odd, core, y, x]).astype(jnp.int32)
    scalars = (pair_list.T, pair_count, here)
    tail = -eigenvalues.shape[0] % TILE
    own_rows = eigenvalues.T
    left, right, across = (shift(own_rows, by, True) for by in (1, -1, 2))
    merge = lambda *rows: jnp.pad(
        jnp.concatenate(rows, axis=0), ((0, 0), (0, tail)), constant_values=1
    )
    top, bottom = merge(own_rows, left), merge(right, across)

    half = query_out.shape[0] // 2
    share = half // parts
    part_in = jnp.dot(
        lax.dynamic_slice_in_dim(query_in, core * half, half, 0), basis_in,
        preferred_element_type=jnp.float32,
    )
    part_out = jnp.dot(
        lax.dynamic_slice_in_dim(query_out, odd * half, half, 0), basis_out,
        preferred_element_type=jnp.float32,
    )
    partial = jnp.concatenate([part_in, jnp.pad(part_out, ((0, 0), (0, tail)))], axis=1)
    width = partial.shape[1]
    sent = (partial * SCALE).astype(jnp.float16).reshape(parts, share, width)
    received = lax.all_to_all(sent, "doc", 0, 0)
    summed = (jnp.sum(received.astype(jnp.float32), axis=0) * (1.0 / SCALE)).astype(jnp.bfloat16)

    doc_rows = jnp.pad(doc_out.reshape(-1, doc_out.shape[2]), ((0, 0), (0, tail)))
    in_rows = doc_in.reshape(-1, model)
    doc_side = arrange(here, in_rows, in_rows, lambda i, _: (0, 0), lambda i, _: (1, 0), model, False)
    after = [shift(rows, 1, False) for rows in (top, bottom)]
    before = [shift(rows, -1, False) for rows in (top, bottom)]

    copies = jnp.broadcast_to(summed[None], (parts, share, width))
    own = lax.all_to_all(copies, "doc", 0, 0).reshape(half, width)
    swap = lambda axis: [(i, i ^ 1) for i in range(lax.axis_size(axis))]
    far_out = lax.ppermute(own[:, model:], "query", swap("query"))
    far_in = lax.ppermute(own[:, :model], "layer", swap("layer"))

    last = [shift(after[0], 1, False), shift(before[1], -1, False)]
    eigen = [top, bottom, *after, *before, *last]
    spread = tuple(number // 2 for number in range(len(eigen)))
    query_side = arrange(here, own, far_in, lambda i, _: (0, 0), lambda i, _: (0, 0), model, True)
    sums = slot_scores(scalars, own, query_side, doc_side, doc_rows, eigen[:-2], spread[:-2])
    scores = slot_scores(
        scalars, own, query_side, doc_side, doc_rows, eigen, spread, (far_out, sums)
    )
    group = lax.axis_size("layer") * lax.axis_size("query")
    copies = jnp.broadcast_to(scores[None], (group,) + scores.shape)
    total = jnp.sum(lax.all_to_all(copies, ("layer", "query"), 0, 0), axis=0)
    return total[:, :DOC_BLOCK].reshape(pair_list.shape[0], QUERY_BLOCK * DOC_BLOCK)


def solution(mesh):
    in_specs = (
        P(None, "doc"),
        P(None, "doc"),
        P("doc", "layer"),
        P("doc", "query"),
        P("layer", ("query", "doc")),
        P("doc", None, "layer"),
        P("doc", None, "query"),
        P("doc", None),
        P("doc"),
    )
    out_specs = P("doc", None)
    return jax.shard_map(local, mesh=mesh, in_specs=in_specs, out_specs=out_specs, check_vma=False)
```

profile of v0, /device:TPU:11, one launch (start us, length us, event | category | flops | bytes accessed | tf_op | source)
XLA Modules:
  0.0 111.1 jit_solution(4565627746006304846)
XLA Ops:
  0.0 0.0 copy-start
  0.0 3.0 %fusion.7 = f32[128,2752]{1,0:T(8,128)S(1)} fusion(bf16[688,2752]{1,0:T(8,128)(2,1)} %param.11, bf16[256,688]{0,1:T(8,128)(2,1)} %param.9, s32[]{:T(128)S(6)} %select_n.30), kind=kOutput, calls=%fused_computation.12 | convolution fusion | flops 484704256 | bytes 5459972
  3.0 0.0 copy-start.6
  3.0 0.1 pad_bitcast_fusion
  3.1 0.0 copy-done
  3.1 0.8 copy-done.6
  3.9 0.2 convolution_bitcast_fusion
  4.2 1.1 %fusion = f16[16,8,3840]{2,1,0:T(8,128)(2,1)} fusion(f32[16,8,2816]{2,1,0:T(8,128)S(1)} %pad_bitcast_fusion, f32[16,8,1024]{2,1,0:T(8,128)S(1)} %convolution_bitcast_fusion), kind=kLoop, calls=%fused_computation.1 | loop fusion | flops 1474560 | bytes 2949120 | tf_op jit(solution)/shard_map/convert_element_type | solution.py:277
  5.3 0.0 copy-start.4
  5.3 6.9 %all-to-all-start = ((f16[16,8,3840]{2,1,0:T(8,128)(2,1)}), f16[16,8,3840]{2,1,0:T(8,128)(2,1)S(1)}, u32[]{:S(2)}, u32[]{:S(2)}) async-start(f16[16,8,3840]{2,1,0:T(8,128)(2,1)} %fusion), calls=%async_computation | async-start | bytes 1966080 | tf_op jit(solution)/shard_map/all_to_all | solution.py:278
  12.2 0.0 copy-done.4
  12.2 1.9 %collective-permute-start.4 = (bf16[64,2752]{1,0:T(8,128)(2,1)S(1)}, bf16[64,2752]{1,0:T(8,128)(2,1)S(1)}, u32[]{:S(2)}, u32[]{:S(2)}) collective-permute-start(bf16[64,2752]{1,0:T(8,128)(2,1)S(1)} %bitcast.26), channel_id=1, source_target_pairs={{0,2},{1,3},{2,0},{3,1},{4,6},{5,7},{6,4},{7,5},{8,10},{9,11},{10,... | collective-permute-start | bytes 1056776 | tf_op jit(solution)/shard_map/ppermute | solution.py:253
  14.1 1.2 %collective-permute-start.3 = (bf16[64,2752]{1,0:T(8,128)(2,1)S(1)}, bf16[64,2752]{1,0:T(8,128)(2,1)}, u32[]{:S(2)}, u32[]{:S(2)}) collective-permute-start(bf16[64,2752]{1,0:T(8,128)(2,1)S(1)} %bitcast.27), channel_id=1, source_target_pairs={{0,3},{1,0},{2,1},{3,2},{4,7},{5,4},{6,5},{7,6},{8,11},{9,8},{10,9... | collective-permute-start | bytes 1056776 | tf_op jit(solution)/shard_map/ppermute | solution.py:253
  15.3 0.3 collective-permute-start.2
  15.6 9.0 %all-to-all-done = f16[16,8,3840]{2,1,0:T(8,128)(2,1)S(1)} async-done(((f16[16,8,3840]{2,1,0:T(8,128)(2,1)}), f16[16,8,3840]{2,1,0:T(8,128)(2,1)S(1)}, u32[]{:S(2)}, u32[]{:S(2)}) %all-to-all-start) | async-done | bytes 983072 | tf_op jit(solution)/shard_map/all_to_all | solution.py:278
  24.6 0.1 convert_reduce_fusion
  24.7 1.0 broadcast_in_dim.4
  25.8 10.3 %all-to-all-start.1 = ((bf16[16,8,3840]{2,1,0:T(8,128)(2,1)}), bf16[16,8,3840]{2,1,0:T(8,128)(2,1)S(1)}, u32[]{:S(2)}, u32[]{:S(2)}) async-start(bf16[16,8,3840]{2,1,0:T(8,128)(2,1)} %broadcast_in_dim.4), calls=%async_computation.1 | async-start | bytes 1966080 | tf_op jit(solution)/shard_map/all_to_all | solution.py:288
  36.1 0.0 copy-start.1
  36.1 0.0 collective-permute-done.2
  36.1 1.1 fusion.5.refs_7_.refs_9_
  37.2 1.3 %collective-permute-start.5 = (bf16[128,2816]{1,0:T(8,128)(2,1)S(1)}, bf16[128,2816]{1,0:T(8,128)(2,1)}, u32[]{:S(2)}, u32[]{:S(2)}) collective-permute-start(bf16[128,2816]{1,0:T(8,128)(2,1)S(1)} %fusion.5.refs_7_.refs_9_), channel_id=1, source_target_pairs={{0,4},{1,5},{2,6},{3,7},{4,8},{5,9},{6,10},{7,11},{8,12},{9,13},{1... | collective-permute-start | bytes 2162696 | tf_op jit(solution)/shard_map/ppermute | solution.py:253
  38.5 0.0 collective-permute-done.4
  38.5 0.0 copy-start.5
  38.5 0.7 copy-done.5
  39.2 0.0 collective-permute-done.3
  39.2 1.2 %fusion.6.refs_8_.refs_10_ = bf16[128,2816]{1,0:T(8,128)(2,1)S(1)} fusion(bf16[64,2752]{1,0:T(8,128)(2,1)} %copy-done.5, bf16[64,2752]{1,0:T(8,128)(2,1)} %collective-permute-done.3), kind=kLoop, calls=%fused_computation.11 | loop fusion | flops 2523136 | bytes 1425408 | tf_op jit(solution)/shard_map/concatenate | solution.py:261
  40.3 0.4 collective-permute-start.8
  40.7 1.5 %collective-permute-start.7 = (bf16[128,2816]{1,0:T(8,128)(2,1)S(1)}, bf16[128,2816]{1,0:T(8,128)(2,1)}, u32[]{:S(2)}, u32[]{:S(2)}) collective-permute-start(bf16[128,2816]{1,0:T(8,128)(2,1)S(1)} %fusion.5.refs_7_.refs_9_), channel_id=1, source_target_pairs={{0,12},{1,13},{2,14},{3,15},{4,0},{5,1},{6,2},{7,3},{8,4},{9,5},{1... | collective-permute-start | bytes 2162696 | tf_op jit(solution)/shard_map/ppermute | solution.py:253
  42.2 0.0 collective-permute-start.6
  42.2 6.0 %all-to-all-done.1 = bf16[16,8,3840]{2,1,0:T(8,128)(2,1)S(1)} async-done(((bf16[16,8,3840]{2,1,0:T(8,128)(2,1)}), bf16[16,8,3840]{2,1,0:T(8,128)(2,1)S(1)}, u32[]{:S(2)}, u32[]{:S(2)}) %all-to-all-start.1) | async-done | bytes 983072 | tf_op jit(solution)/shard_map/all_to_all | solution.py:288
  48.2 0.7 slice.13
  48.9 3.7 %collective-permute-start.1 = (bf16[128,1024]{1,0:T(8,128)(2,1)}, bf16[128,1024]{1,0:T(8,128)(2,1)}, u32[]{:S(2)}, u32[]{:S(2)}) collective-permute-start(bf16[128,1024]{1,0:T(8,128)(2,1)} %slice.13), channel_id=1, source_target_pairs={{0,64},{64,0},{128,192},{192,128},{1,65},{65,1},{129,193},{193,129... | collective-permute-start | bytes 786440 | tf_op jit(solution)/shard_map/ppermute | solution.py:291
  53.3 0.0 copy-start.3
  53.3 0.1 pad_add_fusion.refs_0_.refs_2_
  53.4 0.0 copy-done.1
  53.4 0.8 shard_map.92.refs_5_.refs_7_
  54.2 0.5 copy-done.3
  54.7 0.1 pad.16.refs_6_.refs_8_
  54.8 0.0 copy-start.2
  54.8 1.4 %collective-permute-done.5.refs_9_.refs_11_ = bf16[128,2816]{1,0:T(8,128)(2,1)} collective-permute-done((bf16[128,2816]{1,0:T(8,128)(2,1)S(1)}, bf16[128,2816]{1,0:T(8,128)(2,1)}, u32[]{:S(2)}, u32[]{:S(2)}) %collective-permute-start.5) | collective-permute-done | bytes 720928 | tf_op jit(solution)/shard_map/ppermute | solution.py:253
  56.2 1.1 %collective-permute-start.9 = (bf16[128,2816]{1,0:T(8,128)(2,1)}, bf16[128,2816]{1,0:T(8,128)(2,1)S(1)}, u32[]{:S(2)}, u32[]{:S(2)}) collective-permute-start(bf16[128,2816]{1,0:T(8,128)(2,1)} %collective-permute-done.5.refs_9_.refs_11_), channel_id=1, source_target_pairs={{0,4},{1,5},{2,6},{3,7},{4,8},{5,9},{6,10},{7,11},{8,12},{9,13},{1... | collective-permute-start | bytes 2162696 | tf_op jit(solution)/shard_map/ppermute | solution.py:253
  57.3 0.0 collective-permute-done.8.refs_12_.refs_14_
  57.4 0.9 collective-permute-start.10
  58.3 0.0 collective-permute-done.1.refs_2_
  58.3 1.9 %collective-permute-start = (bf16[128,2816]{1,0:T(8,128)(2,1)S(1)}, bf16[128,2816]{1,0:T(8,128)(2,1)S(1)}, u32[]{:S(2)}, u32[]{:S(2)}) collective-permute-start(bf16[128,2816]{1,0:T(8,128)(2,1)S(1)} %slice.12), channel_id=1, source_target_pairs={{0,16},{16,0},{32,48},{48,32},{1,17},{17,1},{33,49},{49,33},{2,18}... | collective-permute-start | bytes 2162696 | tf_op jit(solution)/shard_map/ppermute | solution.py:290
  60.2 1.8 %shard_map.91.refs_4_.refs_6_ = bf16[1024,256]{1,0:T(8,128)(2,1)S(1)} custom-call(s32[4]{0:T(128)S(1)} %pad_add_fusion.refs_0_.refs_2_, bf16[128,3840]{1,0:T(8,128)(2,1)S(1)} %bitcast.18, bf16[128,1024]{1,0:T(8,128)(2,1)} %collective-permute-done.1.refs_2_), custom_call_target="tpu_custom_call" | custom-call | bytes 1048576 | tf_op jit(solution)/shard_map/pallas_call | solution.py:44
  62.0 2.8 %collective-permute-done.7.refs_11_.refs_13_ = bf16[128,2816]{1,0:T(8,128)(2,1)} collective-permute-done((bf16[128,2816]{1,0:T(8,128)(2,1)S(1)}, bf16[128,2816]{1,0:T(8,128)(2,1)}, u32[]{:S(2)}, u32[]{:S(2)}) %collective-permute-start.7) | collective-permute-done | bytes 720928 | tf_op jit(solution)/shard_map/ppermute | solution.py:253
  64.8 0.0 collective-permute-done.6.refs_10_.refs_12_
  64.8 0.0 copy-done.2
  64.8 13.0 %shard_map.93.refs_5_ = f32[8,256]{1,0:T(8,128)S(1)} custom-call(s32[2,4]{1,0:T(2,128)S(1)} %bitcast.23, s32[1]{0:T(128)S(6)} %copy.14.refs_1_, s32[4]{0:T(128)S(1)} %pad_add_fusion.refs_0_.refs_2_, bf16[128,3840]{1,0:T(8,128)(2,1)S(1)} %bitcast.19, bf16[1024,256]{1,0:T(8,128)(2,1)S(1)} %shard_map.91.refs_4_.refs_6_, ...), custom_call_target="tpu_custom_call" | custom-call | flops 8858370048 | bytes 12845056 | tf_op jit(solution)/shard_map/pallas_call | solution.py:214
  77.8 0.0 collective-permute-done.9.refs_15_
  77.8 0.0 collective-permute-done.10.refs_16_
  77.8 0.0 collective-permute-done.refs_4_
  77.8 9.3 %shard_map.94 = f32[8,128]{1,0:T(8,128)S(1)} custom-call(s32[2,4]{1,0:T(2,128)S(1)} %bitcast.24, s32[1]{0:T(128)S(6)} %copy.14.refs_1_, s32[4]{0:T(128)S(1)} %pad_add_fusion.refs_0_.refs_2_, bf16[128,3840]{1,0:T(8,128)(2,1)S(1)} %bitcast.20, bf16[128,2816]{1,0:T(8,128)(2,1)S(1)} %collective-permute-done.refs_4_, f32[8,256]{1,0:T(8,128)S(1)} %shard_map.93.refs_5_, ...), custom_call_target="tpu_custom_call" | custom-call | flops 11811160064 | bytes 15728640 | tf_op jit(solution)/shard_map/pallas_call | solution.py:214
  87.1 23.3 %all_to_all.15 = f32[16,8,128]{2,1,0:T(8,128)S(1)} all-to-all(f32[16,8,128]{2,1,0:T(8,128)S(1)} %broadcast_in_dim.5), channel_id=1, replica_groups=mesh['layer'=4,'query'=4,'doc'=16] {'layer','query'}, dimensions={0} | all-to-all | bytes 131072 | tf_op jit(solution)/shard_map/all_to_all | solution.py:303
  110.5 0.7 reshape.23
  (4 shorter events, 0.1 us)
Async XLA Ops:
  0.0 3.1 %copy-start = (bf16[256,1024]{1,0:T(8,128)(2,1)S(1)}, bf16[256,1024]{1,0:T(8,128)(2,1)}, u32[]{:S(2)}) copy-start(bf16[256,1024]{1,0:T(8,128)(2,1)} %param.12) | copy-start | bytes 1572868
  3.0 0.9 copy-start.6
  5.3 6.9 %copy-start.4 = (bf16[2752,64]{0,1:T(8,128)(2,1)S(1)}, bf16[2752,64]{0,1:T(8,128)(2,1)}, u32[]{:S(2)}) copy-start(bf16[2752,64]{0,1:T(8,128)(2,1)} %param.13) | copy-start | bytes 1056772
  5.3 19.3 %all-to-all-start = ((f16[16,8,3840]{2,1,0:T(8,128)(2,1)}), f16[16,8,3840]{2,1,0:T(8,128)(2,1)S(1)}, u32[]{:S(2)}, u32[]{:S(2)}) async-start(f16[16,8,3840]{2,1,0:T(8,128)(2,1)} %fusion), calls=%async_computation | async-start | bytes 1966080 | tf_op jit(solution)/shard_map/all_to_all | solution.py:278
  12.2 26.2 %collective-permute-start.4 = (bf16[64,2752]{1,0:T(8,128)(2,1)S(1)}, bf16[64,2752]{1,0:T(8,128)(2,1)S(1)}, u32[]{:S(2)}, u32[]{:S(2)}) collective-permute-start(bf16[64,2752]{1,0:T(8,128)(2,1)S(1)} %bitcast.26), channel_id=1, source_target_pairs={{0,2},{1,3},{2,0},{3,1},{4,6},{5,7},{6,4},{7,5},{8,10},{9,11},{10,... | collective-permute-start | bytes 1056776 | tf_op jit(solution)/shard_map/ppermute | solution.py:253
  14.1 25.1 %collective-permute-start.3 = (bf16[64,2752]{1,0:T(8,128)(2,1)S(1)}, bf16[64,2752]{1,0:T(8,128)(2,1)}, u32[]{:S(2)}, u32[]{:S(2)}) collective-permute-start(bf16[64,2752]{1,0:T(8,128)(2,1)S(1)} %bitcast.27), channel_id=1, source_target_pairs={{0,3},{1,0},{2,1},{3,2},{4,7},{5,4},{6,5},{7,6},{8,11},{9,8},{10,9... | collective-permute-start | bytes 1056776 | tf_op jit(solution)/shard_map/ppermute | solution.py:253
  15.3 20.8 %collective-permute-start.2 = (bf16[64,2752]{1,0:T(8,128)(2,1)S(1)}, bf16[64,2752]{1,0:T(8,128)(2,1)}, u32[]{:S(2)}, u32[]{:S(2)}) collective-permute-start(bf16[64,2752]{1,0:T(8,128)(2,1)S(1)} %bitcast.28), channel_id=1, source_target_pairs={{0,1},{1,2},{2,3},{3,0},{4,5},{5,6},{6,7},{7,4},{8,9},{9,10},{10,1... | collective-permute-start | bytes 1056776 | tf_op jit(solution)/shard_map/ppermute | solution.py:253
  25.8 22.5 %all-to-all-start.1 = ((bf16[16,8,3840]{2,1,0:T(8,128)(2,1)}), bf16[16,8,3840]{2,1,0:T(8,128)(2,1)S(1)}, u32[]{:S(2)}, u32[]{:S(2)}) async-start(bf16[16,8,3840]{2,1,0:T(8,128)(2,1)} %broadcast_in_dim.4), calls=%async_computation.1 | async-start | bytes 1966080 | tf_op jit(solution)/shard_map/all_to_all | solution.py:288
  36.1 17.3 %copy-start.1 = (bf16[4,64,1024]{2,1,0:T(8,128)(2,1)S(1)}, bf16[4,64,1024]{2,1,0:T(8,128)(2,1)}, u32[]{:S(2)}) copy-start(bf16[4,64,1024]{2,1,0:T(8,128)(2,1)} %param.15) | copy-start | bytes 1572868
  37.2 19.0 %collective-permute-start.5 = (bf16[128,2816]{1,0:T(8,128)(2,1)S(1)}, bf16[128,2816]{1,0:T(8,128)(2,1)}, u32[]{:S(2)}, u32[]{:S(2)}) collective-permute-start(bf16[128,2816]{1,0:T(8,128)(2,1)S(1)} %fusion.5.refs_7_.refs_9_), channel_id=1, source_target_pairs={{0,4},{1,5},{2,6},{3,7},{4,8},{5,9},{6,10},{7,11},{8,12},{9,13},{1... | collective-permute-start | bytes 2162696 | tf_op jit(solution)/shard_map/ppermute | solution.py:253
  38.5 0.7 copy-start.5
  40.3 17.0 %collective-permute-start.8 = (bf16[128,2816]{1,0:T(8,128)(2,1)S(1)}, bf16[128,2816]{1,0:T(8,128)(2,1)}, u32[]{:S(2)}, u32[]{:S(2)}) collective-permute-start(bf16[128,2816]{1,0:T(8,128)(2,1)S(1)} %fusion.6.refs_8_.refs_10_), channel_id=1, source_target_pairs={{0,12},{1,13},{2,14},{3,15},{4,0},{5,1},{6,2},{7,3},{8,4},{9,5},{1... | collective-permute-start | bytes 2162696 | tf_op jit(solution)/shard_map/ppermute | solution.py:253
  40.7 24.1 %collective-permute-start.7 = (bf16[128,2816]{1,0:T(8,128)(2,1)S(1)}, bf16[128,2816]{1,0:T(8,128)(2,1)}, u32[]{:S(2)}, u32[]{:S(2)}) collective-permute-start(bf16[128,2816]{1,0:T(8,128)(2,1)S(1)} %fusion.5.refs_7_.refs_9_), channel_id=1, source_target_pairs={{0,12},{1,13},{2,14},{3,15},{4,0},{5,1},{6,2},{7,3},{8,4},{9,5},{1... | collective-permute-start | bytes 2162696 | tf_op jit(solution)/shard_map/ppermute | solution.py:253
  42.2 22.6 %collective-permute-start.6 = (bf16[128,2816]{1,0:T(8,128)(2,1)S(1)}, bf16[128,2816]{1,0:T(8,128)(2,1)}, u32[]{:S(2)}, u32[]{:S(2)}) collective-permute-start(bf16[128,2816]{1,0:T(8,128)(2,1)S(1)} %fusion.6.refs_8_.refs_10_), channel_id=1, source_target_pairs={{0,4},{1,5},{2,6},{3,7},{4,8},{5,9},{6,10},{7,11},{8,12},{9,13},{1... | collective-permute-start | bytes 2162696 | tf_op jit(solution)/shard_map/ppermute | solution.py:253
  48.9 9.4 %collective-permute-start.1 = (bf16[128,1024]{1,0:T(8,128)(2,1)}, bf16[128,1024]{1,0:T(8,128)(2,1)}, u32[]{:S(2)}, u32[]{:S(2)}) collective-permute-start(bf16[128,1024]{1,0:T(8,128)(2,1)} %slice.13), channel_id=1, source_target_pairs={{0,64},{64,0},{128,192},{192,128},{1,65},{65,1},{129,193},{193,129... | collective-permute-start | bytes 786440 | tf_op jit(solution)/shard_map/ppermute | solution.py:291
  53.3 1.4 %copy-start.3 = (bf16[4,64,2752]{2,1,0:T(8,128)(2,1)S(1)}, bf16[4,64,2752]{2,1,0:T(8,128)(2,1)}, u32[]{:S(2)}) copy-start(bf16[4,64,2752]{2,1,0:T(8,128)(2,1)} %param.14) | copy-start | bytes 4227076
  54.8 10.0 %copy-start.2 = (s32[4,2]{0,1:T(2,128)S(1)}, s32[4,2]{0,1:T(2,128)}, u32[]{:S(2)}) copy-start(s32[4,2]{0,1:T(2,128)} %param.16) | copy-start | bytes 100
  56.2 21.6 %collective-permute-start.9 = (bf16[128,2816]{1,0:T(8,128)(2,1)}, bf16[128,2816]{1,0:T(8,128)(2,1)S(1)}, u32[]{:S(2)}, u32[]{:S(2)}) collective-permute-start(bf16[128,2816]{1,0:T(8,128)(2,1)} %collective-permute-done.5.refs_9_.refs_11_), channel_id=1, source_target_pairs={{0,4},{1,5},{2,6},{3,7},{4,8},{5,9},{6,10},{7,11},{8,12},{9,13},{1... | collective-permute-start | bytes 2162696 | tf_op jit(solution)/shard_map/ppermute | solution.py:253
  57.4 20.5 %collective-permute-start.10 = (bf16[128,2816]{1,0:T(8,128)(2,1)}, bf16[128,2816]{1,0:T(8,128)(2,1)S(1)}, u32[]{:S(2)}, u32[]{:S(2)}) collective-permute-start(bf16[128,2816]{1,0:T(8,128)(2,1)} %collective-permute-done.8.refs_12_.refs_14_), channel_id=1, source_target_pairs={{0,12},{1,13},{2,14},{3,15},{4,0},{5,1},{6,2},{7,3},{8,4},{9,5},{1... | collective-permute-start | bytes 2162696 | tf_op jit(solution)/shard_map/ppermute | solution.py:253
  58.3 19.5 %collective-permute-start = (bf16[128,2816]{1,0:T(8,128)(2,1)S(1)}, bf16[128,2816]{1,0:T(8,128)(2,1)S(1)}, u32[]{:S(2)}, u32[]{:S(2)}) collective-permute-start(bf16[128,2816]{1,0:T(8,128)(2,1)S(1)} %slice.12), channel_id=1, source_target_pairs={{0,16},{16,0},{32,48},{48,32},{1,17},{17,1},{33,49},{49,33},{2,18}... | collective-permute-start | bytes 2162696 | tf_op jit(solution)/shard_map/ppermute | solution.py:290
where the time goes:
time: 112 us; the launch traced here: 111 us
  starting transfers between devices  31.4 us (28%)
  Pallas kernels  24.8 us (22%)
  blocking collectives  23.3 us (21%)
  waiting for transfers between devices  19.3 us (17%)
  local copies, waits for them, and re-layouts  4.65 us (4%)
  other arithmetic  3.61 us (3%)
  matrix products  3.23 us (3%)
    all_to_all x1, blocking collectives, local(): total = jnp.sum(lax.all_to_all(copies, ('layer', 'query'), 0, 0), axis=0)  23.3 us
    pallas_call x2, Pallas kernels, slot_scores(): pl.pallas_call(lambda *refs: score_kernel(*refs, spread=spread, last=last...  22.3 us
    all_to_all x1, starting transfers between devices, local(): own = lax.all_to_all(copies, 'doc', 0, 0).reshape(half, width)  10.3 us
    all_to_all x1, waiting for transfers between devices, local(): received = lax.all_to_all(sent, 'doc', 0, 0)  9.03 us
    ppermute x9, starting transfers between devices, shift(): return lax.ppermute(array, ('layer', 'doc'), pairs)  8.52 us
    all_to_all x1, starting transfers between devices, local(): received = lax.all_to_all(sent, 'doc', 0, 0)  6.94 us
    all_to_all x1, waiting for transfers between devices, local(): own = lax.all_to_all(copies, 'doc', 0, 0).reshape(half, width)  6.03 us
    ppermute x9, waiting for transfers between devices, shift(): return lax.ppermute(array, ('layer', 'doc'), pairs)  4.2 us
  transfers between devices with their start and end apart: 13, of which 4 were waited for; matrix products, arithmetic and copies ran while one was open for 4% of the time, Pallas kernels for 14%

commit v1 on v0

--- a/solution.py
+++ b/solution.py
@@ -62,11 +62,11 @@
         far_ref, earlier_ref, refs = refs[0], refs[1], refs[2:]
     query_ref, doc_ref, doc_rows_ref = refs[:3]
     eigen_refs = refs[3:3 + len(spread)]
-    result_ref, eigen, weights, scaled, total, sems = refs[3 + len(spread):9 + len(spread)]
+    result_ref, eigen, scaled, total, sems = refs[3 + len(spread):8 + len(spread)]
     step = pl.program_id(0)
     padded = doc_rows_ref.shape[1]
     first = own_ref.shape[1] - padded
-    band = weights.shape[0]
+    band = eigen.shape[1]
     bands = max(spread) + 1
     slots = pairs.shape[1]
     blocks = total.shape[0] // QUERY_BLOCK
@@ -105,9 +105,7 @@
             if which + 1 < bands:
                 fetch(which + 1, True)
 
-    shifted = eigen[lax.rem(step, 2)].astype(jnp.float32) + damping
-    guess = pl.reciprocal(shifted, approx=True)
-    weights[...] = guess * (2.0 - shifted * guess)
+    arrived = lax.rem(step, 2)
     query_side = query_ref[...]
     doc_side = doc_ref[...].astype(jnp.float32)
     lane = lax.broadcasted_iota(jnp.int32, query_side.shape, 1) // FACTOR_RANK
@@ -127,9 +125,12 @@
             product = jnp.dot(
                 left, rows[:, first + begin:first + end], preferred_element_type=jnp.float32
             )
+            shifted = eigen[arrived, :, begin:end].astype(jnp.float32) + damping
+            guess = pl.reciprocal(shifted, approx=True)
+            weights = guess * (2.0 - shifted * guess)
             for q in range(parts):
                 part = slice(q * band, (q + 1) * band)
-                scaled[part, begin:end] = (product[part] * weights[:, begin:end]).astype(jnp.bfloat16)
+                scaled[part, begin:end] = (product[part] * weights).astype(jnp.bfloat16)
         mixed = lax.dot_general(
             scaled[:parts * band], doc_rows_ref[...], (((1,), (1,)), ((), ())),
             preferred_element_type=jnp.float32,
@@ -204,7 +205,6 @@
     shape = (out_rows, LANES if last else docs)
     scratch = [
         pltpu.VMEM((2, band, padded), jnp.bfloat16),
-        pltpu.VMEM((band, padded), jnp.float32),
         pltpu.VMEM((2 * QUERY_BLOCK * band, padded), jnp.bfloat16),
         pltpu.VMEM((out_rows, docs), jnp.float32),
         pltpu.SemaphoreType.DMA((len(eigen),)),

time: 112 us -> 111 us (level)
  the two profiles are of different devices: /device:TPU:11 before, /device:TPU:29 now
where the time goes in v1:
time: 111 us; the launch traced here: 108 us
  waiting for transfers between devices  30.9 us (28%)
  starting transfers between devices  25 us (23%)
  Pallas kernels  22.2 us (20%)
  blocking collectives  18 us (16%)
  local copies, waits for them, and re-layouts  4.65 us (4%)
  other arithmetic  3.61 us (3%)
  matrix products  3.23 us (3%)
    pallas_call x2, Pallas kernels, slot_scores(): pl.pallas_call(lambda *refs: score_kernel(*refs, spread=spread, last=last...  19.6 us
    all_to_all x1, blocking collectives, local(): total = jnp.sum(lax.all_to_all(copies, ('layer', 'query'), 0, 0), axis=0)  18 us
    all_to_all x1, waiting for transfers between devices, local(): received = lax.all_to_all(sent, 'doc', 0, 0)  12.4 us
    ppermute x9, waiting for transfers between devices, shift(): return lax.ppermute(array, ('layer', 'doc'), pairs)  9.67 us
    ppermute x9, starting transfers between devices, shift(): return lax.ppermute(array, ('layer', 'doc'), pairs)  8.49 us
    all_to_all x1, waiting for transfers between devices, local(): own = lax.all_to_all(copies, 'doc', 0, 0).reshape(half, width)  6.71 us
    all_to_all x1, starting transfers between devices, local(): received = lax.all_to_all(sent, 'doc', 0, 0)  6.69 us
    all_to_all x1, starting transfers between devices, local(): own = lax.all_to_all(copies, 'doc', 0, 0).reshape(half, width)  6.38 us
  transfers between devices with their start and end apart: 13, of which 7 were waited for; matrix products, arithmetic and copies ran while one was open for 4% of the time, Pallas kernels for 6%

profile of v1, /device:TPU:29, one launch (start us, length us, event | category | flops | bytes accessed | tf_op | source)
XLA Modules:
  0.0 108.5 jit_solution(1680947733393682991)
XLA Ops:
  0.0 0.0 copy-start
  0.0 3.0 %fusion.7 = f32[128,2752]{1,0:T(8,128)S(1)} fusion(bf16[688,2752]{1,0:T(8,128)(2,1)} %param.11, bf16[256,688]{0,1:T(8,128)(2,1)} %param.9, s32[]{:T(128)S(6)} %select_n.30), kind=kOutput, calls=%fused_computation.12 | convolution fusion | flops 484704256 | bytes 5459972
  3.0 0.0 copy-start.6
  3.0 0.1 pad_bitcast_fusion
  3.1 0.0 copy-done
  3.1 0.8 copy-done.6
  3.9 0.2 convolution_bitcast_fusion
  4.2 1.1 %fusion = f16[16,8,3840]{2,1,0:T(8,128)(2,1)} fusion(f32[16,8,2816]{2,1,0:T(8,128)S(1)} %pad_bitcast_fusion, f32[16,8,1024]{2,1,0:T(8,128)S(1)} %convolution_bitcast_fusion), kind=kLoop, calls=%fused_computation.1 | loop fusion | flops 1474560 | bytes 2949120 | tf_op jit(solution)/shard_map/convert_element_type | solution.py:277
  5.3 0.0 copy-start.4
  5.3 6.7 %all-to-all-start = ((f16[16,8,3840]{2,1,0:T(8,128)(2,1)}), f16[16,8,3840]{2,1,0:T(8,128)(2,1)S(1)}, u32[]{:S(2)}, u32[]{:S(2)}) async-start(f16[16,8,3840]{2,1,0:T(8,128)(2,1)} %fusion), calls=%async_computation | async-start | bytes 1966080 | tf_op jit(solution)/shard_map/all_to_all | solution.py:278
  12.0 0.0 copy-done.4
  12.0 1.3 %collective-permute-start.4 = (bf16[64,2752]{1,0:T(8,128)(2,1)S(1)}, bf16[64,2752]{1,0:T(8,128)(2,1)S(1)}, u32[]{:S(2)}, u32[]{:S(2)}) collective-permute-start(bf16[64,2752]{1,0:T(8,128)(2,1)S(1)} %bitcast.26), channel_id=1, source_target_pairs={{0,2},{1,3},{2,0},{3,1},{4,6},{5,7},{6,4},{7,5},{8,10},{9,11},{10,... | collective-permute-start | bytes 1056776 | tf_op jit(solution)/shard_map/ppermute | solution.py:253
  13.2 0.0 collective-permute-start.3
  13.2 2.7 %collective-permute-start.2 = (bf16[64,2752]{1,0:T(8,128)(2,1)S(1)}, bf16[64,2752]{1,0:T(8,128)(2,1)}, u32[]{:S(2)}, u32[]{:S(2)}) collective-permute-start(bf16[64,2752]{1,0:T(8,128)(2,1)S(1)} %bitcast.28), channel_id=1, source_target_pairs={{0,1},{1,2},{2,3},{3,0},{4,5},{5,6},{6,7},{7,4},{8,9},{9,10},{10,1... | collective-permute-start | bytes 1056776 | tf_op jit(solution)/shard_map/ppermute | solution.py:253
  15.9 12.4 %all-to-all-done = f16[16,8,3840]{2,1,0:T(8,128)(2,1)S(1)} async-done(((f16[16,8,3840]{2,1,0:T(8,128)(2,1)}), f16[16,8,3840]{2,1,0:T(8,128)(2,1)S(1)}, u32[]{:S(2)}, u32[]{:S(2)}) %all-to-all-start) | async-done | bytes 983072 | tf_op jit(solution)/shard_map/all_to_all | solution.py:278
  28.3 0.1 convert_reduce_fusion
  28.4 1.0 broadcast_in_dim.4
  29.4 6.4 %all-to-all-start.1 = ((bf16[16,8,3840]{2,1,0:T(8,128)(2,1)}), bf16[16,8,3840]{2,1,0:T(8,128)(2,1)S(1)}, u32[]{:S(2)}, u32[]{:S(2)}) async-start(bf16[16,8,3840]{2,1,0:T(8,128)(2,1)} %broadcast_in_dim.4), calls=%async_computation.1 | async-start | bytes 1966080 | tf_op jit(solution)/shard_map/all_to_all | solution.py:288
  35.8 0.0 copy-start.1
  35.8 0.0 collective-permute-done.2
  35.8 1.1 %fusion.5.refs_7_.refs_9_ = bf16[128,2816]{1,0:T(8,128)(2,1)S(1)} fusion(bf16[64,2752]{1,0:T(8,128)(2,1)} %collective-permute-done.2, bf16[64,2752]{1,0:T(8,128)(2,1)S(1)} %bitcast.29), kind=kLoop, calls=%fused_computation.10 | loop fusion | flops 2523136 | bytes 1425408 | tf_op jit(solution)/shard_map/concatenate | solution.py:261
  36.9 1.0 collective-permute-start.5
  37.9 0.0 collective-permute-done.4
  37.9 0.0 copy-start.5
  37.9 0.7 copy-done.5
  38.6 0.0 collective-permute-done.3
  38.6 1.2 %fusion.6.refs_8_.refs_10_ = bf16[128,2816]{1,0:T(8,128)(2,1)S(1)} fusion(bf16[64,2752]{1,0:T(8,128)(2,1)} %copy-done.5, bf16[64,2752]{1,0:T(8,128)(2,1)} %collective-permute-done.3), kind=kLoop, calls=%fused_computation.11 | loop fusion | flops 2523136 | bytes 1425408 | tf_op jit(solution)/shard_map/concatenate | solution.py:261
  39.8 0.7 collective-permute-start.8
  40.5 0.3 collective-permute-start.7
  40.7 1.2 %collective-permute-start.6 = (bf16[128,2816]{1,0:T(8,128)(2,1)S(1)}, bf16[128,2816]{1,0:T(8,128)(2,1)}, u32[]{:S(2)}, u32[]{:S(2)}) collective-permute-start(bf16[128,2816]{1,0:T(8,128)(2,1)S(1)} %fusion.6.refs_8_.refs_10_), channel_id=1, source_target_pairs={{0,4},{1,5},{2,6},{3,7},{4,8},{5,9},{6,10},{7,11},{8,12},{9,13},{1... | collective-permute-start | bytes 2162696 | tf_op jit(solution)/shard_map/ppermute | solution.py:253
  41.9 6.7 %all-to-all-done.1 = bf16[16,8,3840]{2,1,0:T(8,128)(2,1)S(1)} async-done(((bf16[16,8,3840]{2,1,0:T(8,128)(2,1)}), bf16[16,8,3840]{2,1,0:T(8,128)(2,1)S(1)}, u32[]{:S(2)}, u32[]{:S(2)}) %all-to-all-start.1) | async-done | bytes 983072 | tf_op jit(solution)/shard_map/all_to_all | solution.py:288
  48.6 0.7 slice.13
  49.3 1.6 %collective-permute-start.1 = (bf16[128,1024]{1,0:T(8,128)(2,1)}, bf16[128,1024]{1,0:T(8,128)(2,1)}, u32[]{:S(2)}, u32[]{:S(2)}) collective-permute-start(bf16[128,1024]{1,0:T(8,128)(2,1)} %slice.13), channel_id=1, source_target_pairs={{0,64},{64,0},{128,192},{192,128},{1,65},{65,1},{129,193},{193,129... | collective-permute-start | bytes 786440 | tf_op jit(solution)/shard_map/ppermute | solution.py:291
  51.6 0.0 copy-start.3
  51.6 0.1 pad_add_fusion.refs_0_.refs_2_
  51.7 0.0 copy-done.1
  51.7 0.8 shard_map.92.refs_5_.refs_7_
  52.5 0.5 copy-done.3
  52.9 0.1 pad.16.refs_6_.refs_8_
  53.0 0.0 copy-start.2
  53.1 2.9 %collective-permute-done.5.refs_9_.refs_11_ = bf16[128,2816]{1,0:T(8,128)(2,1)} collective-permute-done((bf16[128,2816]{1,0:T(8,128)(2,1)S(1)}, bf16[128,2816]{1,0:T(8,128)(2,1)}, u32[]{:S(2)}, u32[]{:S(2)}) %collective-permute-start.5) | collective-permute-done | bytes 720928 | tf_op jit(solution)/shard_map/ppermute | solution.py:253
  55.9 1.2 %collective-permute-start.9 = (bf16[128,2816]{1,0:T(8,128)(2,1)}, bf16[128,2816]{1,0:T(8,128)(2,1)S(1)}, u32[]{:S(2)}, u32[]{:S(2)}) collective-permute-start(bf16[128,2816]{1,0:T(8,128)(2,1)} %collective-permute-done.5.refs_9_.refs_11_), channel_id=1, source_target_pairs={{0,4},{1,5},{2,6},{3,7},{4,8},{5,9},{6,10},{7,11},{8,12},{9,13},{1... | collective-permute-start | bytes 2162696 | tf_op jit(solution)/shard_map/ppermute | solution.py:253
  57.1 0.0 collective-permute-done.8.refs_12_.refs_14_
  57.1 0.2 collective-permute-start.10
  57.4 0.0 collective-permute-done.1.refs_2_
  57.4 1.9 %collective-permute-start = (bf16[128,2816]{1,0:T(8,128)(2,1)S(1)}, bf16[128,2816]{1,0:T(8,128)(2,1)S(1)}, u32[]{:S(2)}, u32[]{:S(2)}) collective-permute-start(bf16[128,2816]{1,0:T(8,128)(2,1)S(1)} %slice.12), channel_id=1, source_target_pairs={{0,16},{16,0},{32,48},{48,32},{1,17},{17,1},{33,49},{49,33},{2,18}... | collective-permute-start | bytes 2162696 | tf_op jit(solution)/shard_map/ppermute | solution.py:290
  59.3 1.8 %shard_map.91.refs_4_.refs_6_ = bf16[1024,256]{1,0:T(8,128)(2,1)S(1)} custom-call(s32[4]{0:T(128)S(1)} %pad_add_fusion.refs_0_.refs_2_, bf16[128,3840]{1,0:T(8,128)(2,1)S(1)} %bitcast.18, bf16[128,1024]{1,0:T(8,128)(2,1)} %collective-permute-done.1.refs_2_), custom_call_target="tpu_custom_call" | custom-call | bytes 1048576 | tf_op jit(solution)/shard_map/pallas_call | solution.py:44
  61.1 3.2 %collective-permute-done.7.refs_11_.refs_13_ = bf16[128,2816]{1,0:T(8,128)(2,1)} collective-permute-done((bf16[128,2816]{1,0:T(8,128)(2,1)S(1)}, bf16[128,2816]{1,0:T(8,128)(2,1)}, u32[]{:S(2)}, u32[]{:S(2)}) %collective-permute-start.7) | collective-permute-done | bytes 720928 | tf_op jit(solution)/shard_map/ppermute | solution.py:253
  64.3 0.0 collective-permute-done.6.refs_10_.refs_12_
  64.3 0.0 copy-done.2
  64.3 4.0 %shard_map.93.refs_5_ = f32[8,256]{1,0:T(8,128)S(1)} custom-call(s32[2,4]{1,0:T(2,128)S(1)} %bitcast.23, s32[1]{0:T(128)S(6)} %copy.14.refs_1_, s32[4]{0:T(128)S(1)} %pad_add_fusion.refs_0_.refs_2_, bf16[128,3840]{1,0:T(8,128)(2,1)S(1)} %bitcast.19, bf16[1024,256]{1,0:T(8,128)(2,1)S(1)} %shard_map.91.refs_4_.refs_6_, ...), custom_call_target="tpu_custom_call" | custom-call | flops 8858370048 | bytes 12845056 | tf_op jit(solution)/shard_map/pallas_call | solution.py:214
  68.2 3.0 %collective-permute-done.9.refs_15_ = bf16[128,2816]{1,0:T(8,128)(2,1)S(1)} collective-permute-done((bf16[128,2816]{1,0:T(8,128)(2,1)}, bf16[128,2816]{1,0:T(8,128)(2,1)S(1)}, u32[]{:S(2)}, u32[]{:S(2)}) %collective-permute-start.9) | collective-permute-done | bytes 720928 | tf_op jit(solution)/shard_map/ppermute | solution.py:253
  71.3 0.6 collective-permute-done.10.refs_16_
  71.9 2.2 %collective-permute-done.refs_4_ = bf16[128,2816]{1,0:T(8,128)(2,1)S(1)} collective-permute-done((bf16[128,2816]{1,0:T(8,128)(2,1)S(1)}, bf16[128,2816]{1,0:T(8,128)(2,1)S(1)}, u32[]{:S(2)}, u32[]{:S(2)}) %collective-permute-start) | collective-permute-done | bytes 720928 | tf_op jit(solution)/shard_map/ppermute | solution.py:290
  74.1 15.7 %shard_map.94 = f32[8,128]{1,0:T(8,128)S(1)} custom-call(s32[2,4]{1,0:T(2,128)S(1)} %bitcast.24, s32[1]{0:T(128)S(6)} %copy.14.refs_1_, s32[4]{0:T(128)S(1)} %pad_add_fusion.refs_0_.refs_2_, bf16[128,3840]{1,0:T(8,128)(2,1)S(1)} %bitcast.20, bf16[128,2816]{1,0:T(8,128)(2,1)S(1)} %collective-permute-done.refs_4_, f32[8,256]{1,0:T(8,128)S(1)} %shard_map.93.refs_5_, ...), custom_call_target="tpu_custom_call" | custom-call | flops 11811160064 | bytes 15728640 | tf_op jit(solution)/shard_map/pallas_call | solution.py:214
  89.8 18.0 %all_to_all.15 = f32[16,8,128]{2,1,0:T(8,128)S(1)} all-to-all(f32[16,8,128]{2,1,0:T(8,128)S(1)} %broadcast_in_dim.5), channel_id=1, replica_groups=mesh['layer'=4,'query'=4,'doc'=16] {'layer','query'}, dimensions={0} | all-to-all | bytes 131072 | tf_op jit(solution)/shard_map/all_to_all | solution.py:303
  107.8 0.7 reshape.23
  (4 shorter events, 0.1 us)
Async XLA Ops:
  0.0 3.1 %copy-start = (bf16[256,1024]{1,0:T(8,128)(2,1)S(1)}, bf16[256,1024]{1,0:T(8,128)(2,1)}, u32[]{:S(2)}) copy-start(bf16[256,1024]{1,0:T(8,128)(2,1)} %param.12) | copy-start | bytes 1572868
  3.0 0.9 copy-start.6
  5.3 6.7 %copy-start.4 = (bf16[2752,64]{0,1:T(8,128)(2,1)S(1)}, bf16[2752,64]{0,1:T(8,128)(2,1)}, u32[]{:S(2)}) copy-start(bf16[2752,64]{0,1:T(8,128)(2,1)} %param.13) | copy-start | bytes 1056772
  5.3 23.0 %all-to-all-start = ((f16[16,8,3840]{2,1,0:T(8,128)(2,1)}), f16[16,8,3840]{2,1,0:T(8,128)(2,1)S(1)}, u32[]{:S(2)}, u32[]{:S(2)}) async-start(f16[16,8,3840]{2,1,0:T(8,128)(2,1)} %fusion), calls=%async_computation | async-start | bytes 1966080 | tf_op jit(solution)/shard_map/all_to_all | solution.py:278
  12.0 25.9 %collective-permute-start.4 = (bf16[64,2752]{1,0:T(8,128)(2,1)S(1)}, bf16[64,2752]{1,0:T(8,128)(2,1)S(1)}, u32[]{:S(2)}, u32[]{:S(2)}) collective-permute-start(bf16[64,2752]{1,0:T(8,128)(2,1)S(1)} %bitcast.26), channel_id=1, source_target_pairs={{0,2},{1,3},{2,0},{3,1},{4,6},{5,7},{6,4},{7,5},{8,10},{9,11},{10,... | collective-permute-start | bytes 1056776 | tf_op jit(solution)/shard_map/ppermute | solution.py:253
  13.2 25.4 %collective-permute-start.3 = (bf16[64,2752]{1,0:T(8,128)(2,1)S(1)}, bf16[64,2752]{1,0:T(8,128)(2,1)}, u32[]{:S(2)}, u32[]{:S(2)}) collective-permute-start(bf16[64,2752]{1,0:T(8,128)(2,1)S(1)} %bitcast.27), channel_id=1, source_target_pairs={{0,3},{1,0},{2,1},{3,2},{4,7},{5,4},{6,5},{7,6},{8,11},{9,8},{10,9... | collective-permute-start | bytes 1056776 | tf_op jit(solution)/shard_map/ppermute | solution.py:253
  13.2 22.6 %collective-permute-start.2 = (bf16[64,2752]{1,0:T(8,128)(2,1)S(1)}, bf16[64,2752]{1,0:T(8,128)(2,1)}, u32[]{:S(2)}, u32[]{:S(2)}) collective-permute-start(bf16[64,2752]{1,0:T(8,128)(2,1)S(1)} %bitcast.28), channel_id=1, source_target_pairs={{0,1},{1,2},{2,3},{3,0},{4,5},{5,6},{6,7},{7,4},{8,9},{9,10},{10,1... | collective-permute-start | bytes 1056776 | tf_op jit(solution)/shard_map/ppermute | solution.py:253
  29.4 19.2 %all-to-all-start.1 = ((bf16[16,8,3840]{2,1,0:T(8,128)(2,1)}), bf16[16,8,3840]{2,1,0:T(8,128)(2,1)S(1)}, u32[]{:S(2)}, u32[]{:S(2)}) async-start(bf16[16,8,3840]{2,1,0:T(8,128)(2,1)} %broadcast_in_dim.4), calls=%async_computation.1 | async-start | bytes 1966080 | tf_op jit(solution)/shard_map/all_to_all | solution.py:288
  35.8 15.8 %copy-start.1 = (bf16[4,64,1024]{2,1,0:T(8,128)(2,1)S(1)}, bf16[4,64,1024]{2,1,0:T(8,128)(2,1)}, u32[]{:S(2)}) copy-start(bf16[4,64,1024]{2,1,0:T(8,128)(2,1)} %param.15) | copy-start | bytes 1572868
  36.9 19.0 %collective-permute-start.5 = (bf16[128,2816]{1,0:T(8,128)(2,1)S(1)}, bf16[128,2816]{1,0:T(8,128)(2,1)}, u32[]{:S(2)}, u32[]{:S(2)}) collective-permute-start(bf16[128,2816]{1,0:T(8,128)(2,1)S(1)} %fusion.5.refs_7_.refs_9_), channel_id=1, source_target_pairs={{0,4},{1,5},{2,6},{3,7},{4,8},{5,9},{6,10},{7,11},{8,12},{9,13},{1... | collective-permute-start | bytes 2162696 | tf_op jit(solution)/shard_map/ppermute | solution.py:253
  37.9 0.7 copy-start.5
  39.8 17.3 %collective-permute-start.8 = (bf16[128,2816]{1,0:T(8,128)(2,1)S(1)}, bf16[128,2816]{1,0:T(8,128)(2,1)}, u32[]{:S(2)}, u32[]{:S(2)}) collective-permute-start(bf16[128,2816]{1,0:T(8,128)(2,1)S(1)} %fusion.6.refs_8_.refs_10_), channel_id=1, source_target_pairs={{0,12},{1,13},{2,14},{3,15},{4,0},{5,1},{6,2},{7,3},{8,4},{9,5},{1... | collective-permute-start | bytes 2162696 | tf_op jit(solution)/shard_map/ppermute | solution.py:253
  40.5 23.8 %collective-permute-start.7 = (bf16[128,2816]{1,0:T(8,128)(2,1)S(1)}, bf16[128,2816]{1,0:T(8,128)(2,1)}, u32[]{:S(2)}, u32[]{:S(2)}) collective-permute-start(bf16[128,2816]{1,0:T(8,128)(2,1)S(1)} %fusion.5.refs_7_.refs_9_), channel_id=1, source_target_pairs={{0,12},{1,13},{2,14},{3,15},{4,0},{5,1},{6,2},{7,3},{8,4},{9,5},{1... | collective-permute-start | bytes 2162696 | tf_op jit(solution)/shard_map/ppermute | solution.py:253
  40.7 23.6 %collective-permute-start.6 = (bf16[128,2816]{1,0:T(8,128)(2,1)S(1)}, bf16[128,2816]{1,0:T(8,128)(2,1)}, u32[]{:S(2)}, u32[]{:S(2)}) collective-permute-start(bf16[128,2816]{1,0:T(8,128)(2,1)S(1)} %fusion.6.refs_8_.refs_10_), channel_id=1, source_target_pairs={{0,4},{1,5},{2,6},{3,7},{4,8},{5,9},{6,10},{7,11},{8,12},{9,13},{1... | collective-permute-start | bytes 2162696 | tf_op jit(solution)/shard_map/ppermute | solution.py:253
  49.3 8.1 %collective-permute-start.1 = (bf16[128,1024]{1,0:T(8,128)(2,1)}, bf16[128,1024]{1,0:T(8,128)(2,1)}, u32[]{:S(2)}, u32[]{:S(2)}) collective-permute-start(bf16[128,1024]{1,0:T(8,128)(2,1)} %slice.13), channel_id=1, source_target_pairs={{0,64},{64,0},{128,192},{192,128},{1,65},{65,1},{129,193},{193,129... | collective-permute-start | bytes 786440 | tf_op jit(solution)/shard_map/ppermute | solution.py:291
  51.6 1.4 %copy-start.3 = (bf16[4,64,2752]{2,1,0:T(8,128)(2,1)S(1)}, bf16[4,64,2752]{2,1,0:T(8,128)(2,1)}, u32[]{:S(2)}) copy-start(bf16[4,64,2752]{2,1,0:T(8,128)(2,1)} %param.14) | copy-start | bytes 4227076
  53.0 11.2 %copy-start.2 = (s32[4,2]{0,1:T(2,128)S(1)}, s32[4,2]{0,1:T(2,128)}, u32[]{:S(2)}) copy-start(s32[4,2]{0,1:T(2,128)} %param.16) | copy-start | bytes 100
  55.9 15.3 %collective-permute-start.9 = (bf16[128,2816]{1,0:T(8,128)(2,1)}, bf16[128,2816]{1,0:T(8,128)(2,1)S(1)}, u32[]{:S(2)}, u32[]{:S(2)}) collective-permute-start(bf16[128,2816]{1,0:T(8,128)(2,1)} %collective-permute-done.5.refs_9_.refs_11_), channel_id=1, source_target_pairs={{0,4},{1,5},{2,6},{3,7},{4,8},{5,9},{6,10},{7,11},{8,12},{9,13},{1... | collective-permute-start | bytes 2162696 | tf_op jit(solution)/shard_map/ppermute | solution.py:253
  57.1 14.8 %collective-permute-start.10 = (bf16[128,2816]{1,0:T(8,128)(2,1)}, bf16[128,2816]{1,0:T(8,128)(2,1)S(1)}, u32[]{:S(2)}, u32[]{:S(2)}) collective-permute-start(bf16[128,2816]{1,0:T(8,128)(2,1)} %collective-permute-done.8.refs_12_.refs_14_), channel_id=1, source_target_pairs={{0,12},{1,13},{2,14},{3,15},{4,0},{5,1},{6,2},{7,3},{8,4},{9,5},{1... | collective-permute-start | bytes 2162696 | tf_op jit(solution)/shard_map/ppermute | solution.py:253
  57.4 16.6 %collective-permute-start = (bf16[128,2816]{1,0:T(8,128)(2,1)S(1)}, bf16[128,2816]{1,0:T(8,128)(2,1)S(1)}, u32[]{:S(2)}, u32[]{:S(2)}) collective-permute-start(bf16[128,2816]{1,0:T(8,128)(2,1)S(1)} %slice.12), channel_id=1, source_target_pairs={{0,16},{16,0},{32,48},{48,32},{1,17},{17,1},{33,49},{49,33},{2,18}... | collective-permute-start | bytes 2162696 | tf_op jit(solution)/shard_map/ppermute | solution.py:290

commit v2 on v1

--- a/solution.py
+++ b/solution.py
@@ -9,6 +9,7 @@
 QUERY_BLOCK = 2
 DOC_BLOCK = 2
 TILE = 256
+CHUNK = 1536
 LANES = 128
 SIDE = 4
 SCALE = 4096.0
@@ -120,6 +121,7 @@
             axis=0,
         )
         parts = len(places) * QUERY_BLOCK
+        mixed = None
         for begin in range(0, padded, TILE):
             end = begin + TILE
             product = jnp.dot(
@@ -131,10 +133,13 @@
             for q in range(parts):
                 part = slice(q * band, (q + 1) * band)
                 scaled[part, begin:end] = (product[part] * weights).astype(jnp.bfloat16)
-        mixed = lax.dot_general(
-            scaled[:parts * band], doc_rows_ref[...], (((1,), (1,)), ((), ())),
-            preferred_element_type=jnp.float32,
-        )
+            if end % CHUNK == 0 or end == padded:
+                chunk = slice((end - 1) // CHUNK * CHUNK, end)
+                more = lax.dot_general(
+                    scaled[:parts * band, chunk], doc_rows_ref[:, chunk], (((1,), (1,)), ((), ())),
+                    preferred_element_type=jnp.float32,
+                )
+                mixed = more if mixed is None else mixed + more
         for q in range(parts):
             part = mixed[q * band:(q + 1) * band] * doc_side
             block = lax.rem(places[q // QUERY_BLOCK] + here[ODD] * (blocks // 2), blocks)

time: 111 us -> 116 us (1.045)
  the two profiles are of different devices: /device:TPU:29 before, /device:TPU:23 now
where the time goes in v2:
time: 116 us
  starting transfers between devices  31.2 us (27%)
  Pallas kernels  28.9 us (25%)
  waiting for transfers between devices  26.2 us (23%)
  blocking collectives  17 us (15%)
  local copies, waits for them, and re-layouts  4.65 us (4%)
  other arithmetic  3.61 us (3%)
  matrix products  3.23 us (3%)
    pallas_call x2, Pallas kernels, slot_scores(): pl.pallas_call(lambda *refs: score_kernel(*refs, spread=spread, last=last...  26.3 us
    all_to_all x1, blocking collectives, local(): total = jnp.sum(lax.all_to_all(copies, ('layer', 'query'), 0, 0), axis=0)  17 us
    all_to_all x1, starting transfers between devices, local(): own = lax.all_to_all(copies, 'doc', 0, 0).reshape(half, width)  10.9 us
    all_to_all x1, waiting for transfers between devices, local(): received = lax.all_to_all(sent, 'doc', 0, 0)  9.62 us
    ppermute x9, starting transfers between devices, shift(): return lax.ppermute(array, ('layer', 'doc'), pairs)  8.23 us
    ppermute x9, waiting for transfers between devices, shift(): return lax.ppermute(array, ('layer', 'doc'), pairs)  8.19 us
    all_to_all x1, starting transfers between devices, local(): received = lax.all_to_all(sent, 'doc', 0, 0)  6.77 us
    all_to_all x1, waiting for transfers between devices, local(): own = lax.all_to_all(copies, 'doc', 0, 0).reshape(half, width)  4.37 us
  transfers between devices with their start and end apart: 13, of which 7 were waited for; matrix products, arithmetic and copies ran while one was open for 4% of the time, Pallas kernels for 6%

profile of v2, /device:TPU:23, one launch (start us, length us, event | category | flops | bytes accessed | tf_op | source)
XLA Modules:
  0.0 115.6 jit_solution(13737122075081667445)
XLA Ops:
  0.0 0.0 copy-start
  0.0 3.0 %fusion.7 = f32[128,2752]{1,0:T(8,128)S(1)} fusion(bf16[688,2752]{1,0:T(8,128)(2,1)} %param.11, bf16[256,688]{0,1:T(8,128)(2,1)} %param.9, s32[]{:T(128)S(6)} %select_n.30), kind=kOutput, calls=%fused_computation.12 | convolution fusion | flops 484704256 | bytes 5459972
  3.0 0.0 copy-start.6
  3.0 0.1 pad_bitcast_fusion
  3.1 0.0 copy-done
  3.1 0.8 copy-done.6
  3.9 0.2 convolution_bitcast_fusion
  4.2 1.1 fusion
  5.3 0.0 copy-start.4
  5.3 6.8 %all-to-all-start = ((f16[16,8,3840]{2,1,0:T(8,128)(2,1)}), f16[16,8,3840]{2,1,0:T(8,128)(2,1)S(1)}, u32[]{:S(2)}, u32[]{:S(2)}) async-start(f16[16,8,3840]{2,1,0:T(8,128)(2,1)} %fusion), calls=%async_computation | async-start | bytes 1966080 | tf_op jit(solution)/shard_map/all_to_all | solution.py:283
  12.0 0.0 copy-done.4
  12.1 0.4 collective-permute-start.4
  12.4 1.8 %collective-permute-start.3 = (bf16[64,2752]{1,0:T(8,128)(2,1)S(1)}, bf16[64,2752]{1,0:T(8,128)(2,1)}, u32[]{:S(2)}, u32[]{:S(2)}) collective-permute-start(bf16[64,2752]{1,0:T(8,128)(2,1)S(1)} %bitcast.27), channel_id=1, source_target_pairs={{0,3},{1,0},{2,1},{3,2},{4,7},{5,4},{6,5},{7,6},{8,11},{9,8},{10,9... | collective-permute-start | bytes 1056776 | tf_op jit(solution)/shard_map/ppermute | solution.py:258
  14.2 0.0 collective-permute-start.2
  14.2 9.6 %all-to-all-done = f16[16,8,3840]{2,1,0:T(8,128)(2,1)S(1)} async-done(((f16[16,8,3840]{2,1,0:T(8,128)(2,1)}), f16[16,8,3840]{2,1,0:T(8,128)(2,1)S(1)}, u32[]{:S(2)}, u32[]{:S(2)}) %all-to-all-start) | async-done | bytes 983072 | tf_op jit(solution)/shard_map/all_to_all | solution.py:283
  23.8 0.1 convert_reduce_fusion
  24.0 1.0 broadcast_in_dim.4
  25.0 10.9 %all-to-all-start.1 = ((bf16[16,8,3840]{2,1,0:T(8,128)(2,1)}), bf16[16,8,3840]{2,1,0:T(8,128)(2,1)S(1)}, u32[]{:S(2)}, u32[]{:S(2)}) async-start(bf16[16,8,3840]{2,1,0:T(8,128)(2,1)} %broadcast_in_dim.4), calls=%async_computation.1 | async-start | bytes 1966080 | tf_op jit(solution)/shard_map/all_to_all | solution.py:293
  35.9 0.0 copy-start.1
  35.9 0.0 collective-permute-done.2
  35.9 1.1 fusion.5.refs_7_.refs_9_
  37.0 0.4 collective-permute-start.5
  37.4 0.0 collective-permute-done.4
  37.4 0.0 copy-start.5
  37.4 0.7 copy-done.5
  38.1 0.0 collective-permute-done.3
  38.1 1.2 fusion.6.refs_8_.refs_10_
  39.3 1.3 %collective-permute-start.8 = (bf16[128,2816]{1,0:T(8,128)(2,1)S(1)}, bf16[128,2816]{1,0:T(8,128)(2,1)}, u32[]{:S(2)}, u32[]{:S(2)}) collective-permute-start(bf16[128,2816]{1,0:T(8,128)(2,1)S(1)} %fusion.6.refs_8_.refs_10_), channel_id=1, source_target_pairs={{0,12},{1,13},{2,14},{3,15},{4,0},{5,1},{6,2},{7,3},{8,4},{9,5},{1... | collective-permute-start | bytes 2162696 | tf_op jit(solution)/shard_map/ppermute | solution.py:258
  40.5 0.6 collective-permute-start.7
  41.1 2.1 %collective-permute-start.6 = (bf16[128,2816]{1,0:T(8,128)(2,1)S(1)}, bf16[128,2816]{1,0:T(8,128)(2,1)}, u32[]{:S(2)}, u32[]{:S(2)}) collective-permute-start(bf16[128,2816]{1,0:T(8,128)(2,1)S(1)} %fusion.6.refs_8_.refs_10_), channel_id=1, source_target_pairs={{0,4},{1,5},{2,6},{3,7},{4,8},{5,9},{6,10},{7,11},{8,12},{9,13},{1... | collective-permute-start | bytes 2162696 | tf_op jit(solution)/shard_map/ppermute | solution.py:258
  43.2 4.4 %all-to-all-done.1 = bf16[16,8,3840]{2,1,0:T(8,128)(2,1)S(1)} async-done(((bf16[16,8,3840]{2,1,0:T(8,128)(2,1)}), bf16[16,8,3840]{2,1,0:T(8,128)(2,1)S(1)}, u32[]{:S(2)}, u32[]{:S(2)}) %all-to-all-start.1) | async-done | bytes 983072 | tf_op jit(solution)/shard_map/all_to_all | solution.py:293
  47.6 0.7 slice.13
  48.3 3.6 %collective-permute-start.1 = (bf16[128,1024]{1,0:T(8,128)(2,1)}, bf16[128,1024]{1,0:T(8,128)(2,1)}, u32[]{:S(2)}, u32[]{:S(2)}) collective-permute-start(bf16[128,1024]{1,0:T(8,128)(2,1)} %slice.13), channel_id=1, source_target_pairs={{0,64},{64,0},{128,192},{192,128},{1,65},{65,1},{129,193},{193,129... | collective-permute-start | bytes 786440 | tf_op jit(solution)/shard_map/ppermute | solution.py:296
  52.5 0.0 copy-start.3
  52.5 0.1 pad_add_fusion.refs_0_.refs_2_
  52.6 0.0 copy-done.1
  52.6 0.8 shard_map.92.refs_5_.refs_7_
  53.4 0.5 copy-done.3
  53.9 0.1 pad.16.refs_6_.refs_8_
  54.0 0.0 copy-start.2
  54.0 2.3 %collective-permute-done.5.refs_9_.refs_11_ = bf16[128,2816]{1,0:T(8,128)(2,1)} collective-permute-done((bf16[128,2816]{1,0:T(8,128)(2,1)S(1)}, bf16[128,2816]{1,0:T(8,128)(2,1)}, u32[]{:S(2)}, u32[]{:S(2)}) %collective-permute-start.5) | collective-permute-done | bytes 720928 | tf_op jit(solution)/shard_map/ppermute | solution.py:258
  56.3 1.8 %collective-permute-start.9 = (bf16[128,2816]{1,0:T(8,128)(2,1)}, bf16[128,2816]{1,0:T(8,128)(2,1)S(1)}, u32[]{:S(2)}, u32[]{:S(2)}) collective-permute-start(bf16[128,2816]{1,0:T(8,128)(2,1)} %collective-permute-done.5.refs_9_.refs_11_), channel_id=1, source_target_pairs={{0,4},{1,5},{2,6},{3,7},{4,8},{5,9},{6,10},{7,11},{8,12},{9,13},{1... | collective-permute-start | bytes 2162696 | tf_op jit(solution)/shard_map/ppermute | solution.py:258
  58.1 0.0 collective-permute-done.8.refs_12_.refs_14_
  58.1 0.0 collective-permute-start.10
  58.2 0.0 collective-permute-done.1.refs_2_
  58.2 1.7 %collective-permute-start = (bf16[128,2816]{1,0:T(8,128)(2,1)S(1)}, bf16[128,2816]{1,0:T(8,128)(2,1)S(1)}, u32[]{:S(2)}, u32[]{:S(2)}) collective-permute-start(bf16[128,2816]{1,0:T(8,128)(2,1)S(1)} %slice.12), channel_id=1, source_target_pairs={{0,16},{16,0},{32,48},{48,32},{1,17},{17,1},{33,49},{49,33},{2,18}... | collective-permute-start | bytes 2162696 | tf_op jit(solution)/shard_map/ppermute | solution.py:295
  59.9 1.8 %shard_map.91.refs_4_.refs_6_ = bf16[1024,256]{1,0:T(8,128)(2,1)S(1)} custom-call(s32[4]{0:T(128)S(1)} %pad_add_fusion.refs_0_.refs_2_, bf16[128,3840]{1,0:T(8,128)(2,1)S(1)} %bitcast.18, bf16[128,1024]{1,0:T(8,128)(2,1)} %collective-permute-done.1.refs_2_), custom_call_target="tpu_custom_call" | custom-call | bytes 1048576 | tf_op jit(solution)/shard_map/pallas_call | solution.py:45
  61.7 1.8 %collective-permute-done.7.refs_11_.refs_13_ = bf16[128,2816]{1,0:T(8,128)(2,1)} collective-permute-done((bf16[128,2816]{1,0:T(8,128)(2,1)S(1)}, bf16[128,2816]{1,0:T(8,128)(2,1)}, u32[]{:S(2)}, u32[]{:S(2)}) %collective-permute-start.7) | collective-permute-done | bytes 720928 | tf_op jit(solution)/shard_map/ppermute | solution.py:258
  63.4 0.6 collective-permute-done.6.refs_10_.refs_12_
  64.1 0.0 copy-done.2
  64.1 4.1 %shard_map.93.refs_5_ = f32[8,256]{1,0:T(8,128)S(1)} custom-call(s32[2,4]{1,0:T(2,128)S(1)} %bitcast.23, s32[1]{0:T(128)S(6)} %copy.14.refs_1_, s32[4]{0:T(128)S(1)} %pad_add_fusion.refs_0_.refs_2_, bf16[128,3840]{1,0:T(8,128)(2,1)S(1)} %bitcast.19, bf16[1024,256]{1,0:T(8,128)(2,1)S(1)} %shard_map.91.refs_4_.refs_6_, ...), custom_call_target="tpu_custom_call" | custom-call | flops 8858370048 | bytes 12845056 | tf_op jit(solution)/shard_map/pallas_call | solution.py:219
  68.2 3.5 %collective-permute-done.9.refs_15_ = bf16[128,2816]{1,0:T(8,128)(2,1)S(1)} collective-permute-done((bf16[128,2816]{1,0:T(8,128)(2,1)}, bf16[128,2816]{1,0:T(8,128)(2,1)S(1)}, u32[]{:S(2)}, u32[]{:S(2)}) %collective-permute-start.9) | collective-permute-done | bytes 720928 | tf_op jit(solution)/shard_map/ppermute | solution.py:258
  71.7 0.0 collective-permute-done.10.refs_16_
  71.7 4.0 %collective-permute-done.refs_4_ = bf16[128,2816]{1,0:T(8,128)(2,1)S(1)} collective-permute-done((bf16[128,2816]{1,0:T(8,128)(2,1)S(1)}, bf16[128,2816]{1,0:T(8,128)(2,1)S(1)}, u32[]{:S(2)}, u32[]{:S(2)}) %collective-permute-start) | collective-permute-done | bytes 720928 | tf_op jit(solution)/shard_map/ppermute | solution.py:295
  75.6 22.2 %shard_map.94 = f32[8,128]{1,0:T(8,128)S(1)} custom-call(s32[2,4]{1,0:T(2,128)S(1)} %bitcast.24, s32[1]{0:T(128)S(6)} %copy.14.refs_1_, s32[4]{0:T(128)S(1)} %pad_add_fusion.refs_0_.refs_2_, bf16[128,3840]{1,0:T(8,128)(2,1)S(1)} %bitcast.20, bf16[128,2816]{1,0:T(8,128)(2,1)S(1)} %collective-permute-done.refs_4_, f32[8,256]{1,0:T(8,128)S(1)} %shard_map.93.refs_5_, ...), custom_call_target="tpu_custom_call" | custom-call | flops 11811160064 | bytes 15728640 | tf_op jit(solution)/shard_map/pallas_call | solution.py:219
  97.9 17.0 %all_to_all.15 = f32[16,8,128]{2,1,0:T(8,128)S(1)} all-to-all(f32[16,8,128]{2,1,0:T(8,128)S(1)} %broadcast_in_dim.5), channel_id=1, replica_groups=mesh['layer'=4,'query'=4,'doc'=16] {'layer','query'}, dimensions={0} | all-to-all | bytes 131072 | tf_op jit(solution)/shard_map/all_to_all | solution.py:308
  114.9 0.7 reshape.23
  (4 shorter events, 0.1 us)
Async XLA Ops:
  0.0 3.1 %copy-start = (bf16[256,1024]{1,0:T(8,128)(2,1)S(1)}, bf16[256,1024]{1,0:T(8,128)(2,1)}, u32[]{:S(2)}) copy-start(bf16[256,1024]{1,0:T(8,128)(2,1)} %param.12) | copy-start | bytes 1572868
  3.0 0.9 copy-start.6
  5.3 6.8 %copy-start.4 = (bf16[2752,64]{0,1:T(8,128)(2,1)S(1)}, bf16[2752,64]{0,1:T(8,128)(2,1)}, u32[]{:S(2)}) copy-start(bf16[2752,64]{0,1:T(8,128)(2,1)} %param.13) | copy-start | bytes 1056772
  5.3 18.6 %all-to-all-start = ((f16[16,8,3840]{2,1,0:T(8,128)(2,1)}), f16[16,8,3840]{2,1,0:T(8,128)(2,1)S(1)}, u32[]{:S(2)}, u32[]{:S(2)}) async-start(f16[16,8,3840]{2,1,0:T(8,128)(2,1)} %fusion), calls=%async_computation | async-start | bytes 1966080 | tf_op jit(solution)/shard_map/all_to_all | solution.py:283
  12.1 25.3 %collective-permute-start.4 = (bf16[64,2752]{1,0:T(8,128)(2,1)S(1)}, bf16[64,2752]{1,0:T(8,128)(2,1)S(1)}, u32[]{:S(2)}, u32[]{:S(2)}) collective-permute-start(bf16[64,2752]{1,0:T(8,128)(2,1)S(1)} %bitcast.26), channel_id=1, source_target_pairs={{0,2},{1,3},{2,0},{3,1},{4,6},{5,7},{6,4},{7,5},{8,10},{9,11},{10,... | collective-permute-start | bytes 1056776 | tf_op jit(solution)/shard_map/ppermute | solution.py:258
  12.4 25.7 %collective-permute-start.3 = (bf16[64,2752]{1,0:T(8,128)(2,1)S(1)}, bf16[64,2752]{1,0:T(8,128)(2,1)}, u32[]{:S(2)}, u32[]{:S(2)}) collective-permute-start(bf16[64,2752]{1,0:T(8,128)(2,1)S(1)} %bitcast.27), channel_id=1, source_target_pairs={{0,3},{1,0},{2,1},{3,2},{4,7},{5,4},{6,5},{7,6},{8,11},{9,8},{10,9... | collective-permute-start | bytes 1056776 | tf_op jit(solution)/shard_map/ppermute | solution.py:258
  14.2 21.7 %collective-permute-start.2 = (bf16[64,2752]{1,0:T(8,128)(2,1)S(1)}, bf16[64,2752]{1,0:T(8,128)(2,1)}, u32[]{:S(2)}, u32[]{:S(2)}) collective-permute-start(bf16[64,2752]{1,0:T(8,128)(2,1)S(1)} %bitcast.28), channel_id=1, source_target_pairs={{0,1},{1,2},{2,3},{3,0},{4,5},{5,6},{6,7},{7,4},{8,9},{9,10},{10,1... | collective-permute-start | bytes 1056776 | tf_op jit(solution)/shard_map/ppermute | solution.py:258
  25.0 22.6 %all-to-all-start.1 = ((bf16[16,8,3840]{2,1,0:T(8,128)(2,1)}), bf16[16,8,3840]{2,1,0:T(8,128)(2,1)S(1)}, u32[]{:S(2)}, u32[]{:S(2)}) async-start(bf16[16,8,3840]{2,1,0:T(8,128)(2,1)} %broadcast_in_dim.4), calls=%async_computation.1 | async-start | bytes 1966080 | tf_op jit(solution)/shard_map/all_to_all | solution.py:293
  35.9 16.7 %copy-start.1 = (bf16[4,64,1024]{2,1,0:T(8,128)(2,1)S(1)}, bf16[4,64,1024]{2,1,0:T(8,128)(2,1)}, u32[]{:S(2)}) copy-start(bf16[4,64,1024]{2,1,0:T(8,128)(2,1)} %param.15) | copy-start | bytes 1572868
  37.0 19.3 %collective-permute-start.5 = (bf16[128,2816]{1,0:T(8,128)(2,1)S(1)}, bf16[128,2816]{1,0:T(8,128)(2,1)}, u32[]{:S(2)}, u32[]{:S(2)}) collective-permute-start(bf16[128,2816]{1,0:T(8,128)(2,1)S(1)} %fusion.5.refs_7_.refs_9_), channel_id=1, source_target_pairs={{0,4},{1,5},{2,6},{3,7},{4,8},{5,9},{6,10},{7,11},{8,12},{9,13},{1... | collective-permute-start | bytes 2162696 | tf_op jit(solution)/shard_map/ppermute | solution.py:258
  37.4 0.7 copy-start.5
  39.3 18.8 %collective-permute-start.8 = (bf16[128,2816]{1,0:T(8,128)(2,1)S(1)}, bf16[128,2816]{1,0:T(8,128)(2,1)}, u32[]{:S(2)}, u32[]{:S(2)}) collective-permute-start(bf16[128,2816]{1,0:T(8,128)(2,1)S(1)} %fusion.6.refs_8_.refs_10_), channel_id=1, source_target_pairs={{0,12},{1,13},{2,14},{3,15},{4,0},{5,1},{6,2},{7,3},{8,4},{9,5},{1... | collective-permute-start | bytes 2162696 | tf_op jit(solution)/shard_map/ppermute | solution.py:258
  40.5 22.9 %collective-permute-start.7 = (bf16[128,2816]{1,0:T(8,128)(2,1)S(1)}, bf16[128,2816]{1,0:T(8,128)(2,1)}, u32[]{:S(2)}, u32[]{:S(2)}) collective-permute-start(bf16[128,2816]{1,0:T(8,128)(2,1)S(1)} %fusion.5.refs_7_.refs_9_), channel_id=1, source_target_pairs={{0,12},{1,13},{2,14},{3,15},{4,0},{5,1},{6,2},{7,3},{8,4},{9,5},{1... | collective-permute-start | bytes 2162696 | tf_op jit(solution)/shard_map/ppermute | solution.py:258
  41.1 22.9 %collective-permute-start.6 = (bf16[128,2816]{1,0:T(8,128)(2,1)S(1)}, bf16[128,2816]{1,0:T(8,128)(2,1)}, u32[]{:S(2)}, u32[]{:S(2)}) collective-permute-start(bf16[128,2816]{1,0:T(8,128)(2,1)S(1)} %fusion.6.refs_8_.refs_10_), channel_id=1, source_target_pairs={{0,4},{1,5},{2,6},{3,7},{4,8},{5,9},{6,10},{7,11},{8,12},{9,13},{1... | collective-permute-start | bytes 2162696 | tf_op jit(solution)/shard_map/ppermute | solution.py:258
  48.3 9.9 %collective-permute-start.1 = (bf16[128,1024]{1,0:T(8,128)(2,1)}, bf16[128,1024]{1,0:T(8,128)(2,1)}, u32[]{:S(2)}, u32[]{:S(2)}) collective-permute-start(bf16[128,1024]{1,0:T(8,128)(2,1)} %slice.13), channel_id=1, source_target_pairs={{0,64},{64,0},{128,192},{192,128},{1,65},{65,1},{129,193},{193,129... | collective-permute-start | bytes 786440 | tf_op jit(solution)/shard_map/ppermute | solution.py:296
  52.5 1.4 %copy-start.3 = (bf16[4,64,2752]{2,1,0:T(8,128)(2,1)S(1)}, bf16[4,64,2752]{2,1,0:T(8,128)(2,1)}, u32[]{:S(2)}) copy-start(bf16[4,64,2752]{2,1,0:T(8,128)(2,1)} %param.14) | copy-start | bytes 4227076
  54.0 10.1 %copy-start.2 = (s32[4,2]{0,1:T(2,128)S(1)}, s32[4,2]{0,1:T(2,128)}, u32[]{:S(2)}) copy-start(s32[4,2]{0,1:T(2,128)} %param.16) | copy-start | bytes 100
  56.3 15.3 %collective-permute-start.9 = (bf16[128,2816]{1,0:T(8,128)(2,1)}, bf16[128,2816]{1,0:T(8,128)(2,1)S(1)}, u32[]{:S(2)}, u32[]{:S(2)}) collective-permute-start(bf16[128,2816]{1,0:T(8,128)(2,1)} %collective-permute-done.5.refs_9_.refs_11_), channel_id=1, source_target_pairs={{0,4},{1,5},{2,6},{3,7},{4,8},{5,9},{6,10},{7,11},{8,12},{9,13},{1... | collective-permute-start | bytes 2162696 | tf_op jit(solution)/shard_map/ppermute | solution.py:258
  58.1 13.6 %collective-permute-start.10 = (bf16[128,2816]{1,0:T(8,128)(2,1)}, bf16[128,2816]{1,0:T(8,128)(2,1)S(1)}, u32[]{:S(2)}, u32[]{:S(2)}) collective-permute-start(bf16[128,2816]{1,0:T(8,128)(2,1)} %collective-permute-done.8.refs_12_.refs_14_), channel_id=1, source_target_pairs={{0,12},{1,13},{2,14},{3,15},{4,0},{5,1},{6,2},{7,3},{8,4},{9,5},{1... | collective-permute-start | bytes 2162696 | tf_op jit(solution)/shard_map/ppermute | solution.py:258
  58.2 17.5 %collective-permute-start = (bf16[128,2816]{1,0:T(8,128)(2,1)S(1)}, bf16[128,2816]{1,0:T(8,128)(2,1)S(1)}, u32[]{:S(2)}, u32[]{:S(2)}) collective-permute-start(bf16[128,2816]{1,0:T(8,128)(2,1)S(1)} %slice.12), channel_id=1, source_target_pairs={{0,16},{16,0},{32,48},{48,32},{1,17},{17,1},{33,49},{49,33},{2,18}... | collective-permute-start | bytes 2162696 | tf_op jit(solution)/shard_map/ppermute | solution.py:295

commit v3 on v1

--- a/solution.py
+++ b/solution.py
@@ -120,8 +120,8 @@
             axis=0,
         )
         parts = len(places) * QUERY_BLOCK
-        for begin in range(0, padded, TILE):
-            end = begin + TILE
+        for begin in range(0, padded, 2 * TILE):
+            end = min(begin + 2 * TILE, padded)
             product = jnp.dot(
                 left, rows[:, first + begin:first + end], preferred_element_type=jnp.float32
             )

time: 111 us -> 113 us (1.018)
  the two profiles are of different devices: /device:TPU:29 before, /device:TPU:1 now
where the time goes in v3:
time: 113 us
  starting transfers between devices  32.2 us (28%)
  waiting for transfers between devices  28.6 us (25%)
  Pallas kernels  22.2 us (20%)
  blocking collectives  17.7 us (16%)
  local copies, waits for them, and re-layouts  4.65 us (4%)
  other arithmetic  3.61 us (3%)
  matrix products  3.23 us (3%)
    pallas_call x2, Pallas kernels, slot_scores(): pl.pallas_call(lambda *refs: score_kernel(*refs, spread=spread, last=last...  19.6 us
    all_to_all x1, blocking collectives, local(): total = jnp.sum(lax.all_to_all(copies, ('layer', 'query'), 0, 0), axis=0)  17.7 us
    ppermute x9, starting transfers between devices, shift(): return lax.ppermute(array, ('layer', 'doc'), pairs)  11.4 us
    all_to_all x1, waiting for transfers between devices, local(): received = lax.all_to_all(sent, 'doc', 0, 0)  11.1 us
    all_to_all x1, waiting for transfers between devices, local(): own = lax.all_to_all(copies, 'doc', 0, 0).reshape(half, width)  7.75 us
    all_to_all x1, starting transfers between devices, local(): received = lax.all_to_all(sent, 'doc', 0, 0)  7.72 us
    all_to_all x1, starting transfers between devices, local(): own = lax.all_to_all(copies, 'doc', 0, 0).reshape(half, width)  7.19 us
    ppermute x9, waiting for transfers between devices, shift(): return lax.ppermute(array, ('layer', 'doc'), pairs)  5.44 us
  transfers between devices with their start and end apart: 13, of which 7 were waited for; matrix products, arithmetic and copies ran while one was open for 4% of the time, Pallas kernels for 6%

profile of v3, /device:TPU:1, one launch (start us, length us, event | category | flops | bytes accessed | tf_op | source)
XLA Modules:
  0.0 113.0 jit_solution(1680947733393682991)
XLA Ops:
  0.0 0.0 copy-start
  0.0 3.0 %fusion.7 = f32[128,2752]{1,0:T(8,128)S(1)} fusion(bf16[688,2752]{1,0:T(8,128)(2,1)} %param.11, bf16[256,688]{0,1:T(8,128)(2,1)} %param.9, s32[]{:T(128)S(6)} %select_n.30), kind=kOutput, calls=%fused_computation.12 | convolution fusion | flops 484704256 | bytes 5459972
  3.0 0.0 copy-start.6
  3.0 0.1 pad_bitcast_fusion
  3.1 0.0 copy-done
  3.1 0.8 copy-done.6
  3.9 0.2 convolution_bitcast_fusion
  4.2 1.1 fusion
  5.3 0.0 copy-start.4
  5.3 7.7 %all-to-all-start = ((f16[16,8,3840]{2,1,0:T(8,128)(2,1)}), f16[16,8,3840]{2,1,0:T(8,128)(2,1)S(1)}, u32[]{:S(2)}, u32[]{:S(2)}) async-start(f16[16,8,3840]{2,1,0:T(8,128)(2,1)} %fusion), calls=%async_computation | async-start | bytes 1966080 | tf_op jit(solution)/shard_map/all_to_all | solution.py:278
  13.0 0.0 copy-done.4
  13.0 3.0 %collective-permute-start.4 = (bf16[64,2752]{1,0:T(8,128)(2,1)S(1)}, bf16[64,2752]{1,0:T(8,128)(2,1)S(1)}, u32[]{:S(2)}, u32[]{:S(2)}) collective-permute-start(bf16[64,2752]{1,0:T(8,128)(2,1)S(1)} %bitcast.26), channel_id=1, source_target_pairs={{0,2},{1,3},{2,0},{3,1},{4,6},{5,7},{6,4},{7,5},{8,10},{9,11},{10,... | collective-permute-start | bytes 1056776 | tf_op jit(solution)/shard_map/ppermute | solution.py:253
  16.0 0.9 collective-permute-start.3
  16.9 0.6 collective-permute-start.2
  17.4 11.1 %all-to-all-done = f16[16,8,3840]{2,1,0:T(8,128)(2,1)S(1)} async-done(((f16[16,8,3840]{2,1,0:T(8,128)(2,1)}), f16[16,8,3840]{2,1,0:T(8,128)(2,1)S(1)}, u32[]{:S(2)}, u32[]{:S(2)}) %all-to-all-start) | async-done | bytes 983072 | tf_op jit(solution)/shard_map/all_to_all | solution.py:278
  28.5 0.1 convert_reduce_fusion
  28.6 1.0 broadcast_in_dim.4
  29.7 7.2 %all-to-all-start.1 = ((bf16[16,8,3840]{2,1,0:T(8,128)(2,1)}), bf16[16,8,3840]{2,1,0:T(8,128)(2,1)S(1)}, u32[]{:S(2)}, u32[]{:S(2)}) async-start(bf16[16,8,3840]{2,1,0:T(8,128)(2,1)} %broadcast_in_dim.4), calls=%async_computation.1 | async-start | bytes 1966080 | tf_op jit(solution)/shard_map/all_to_all | solution.py:288
  36.9 0.0 copy-start.1
  36.9 0.0 collective-permute-done.2
  36.9 1.1 fusion.5.refs_7_.refs_9_
  38.0 1.4 %collective-permute-start.5 = (bf16[128,2816]{1,0:T(8,128)(2,1)S(1)}, bf16[128,2816]{1,0:T(8,128)(2,1)}, u32[]{:S(2)}, u32[]{:S(2)}) collective-permute-start(bf16[128,2816]{1,0:T(8,128)(2,1)S(1)} %fusion.5.refs_7_.refs_9_), channel_id=1, source_target_pairs={{0,4},{1,5},{2,6},{3,7},{4,8},{5,9},{6,10},{7,11},{8,12},{9,13},{1... | collective-permute-start | bytes 2162696 | tf_op jit(solution)/shard_map/ppermute | solution.py:253
  39.4 0.0 collective-permute-done.4
  39.4 0.0 copy-start.5
  39.4 0.7 copy-done.5
  40.2 0.0 collective-permute-done.3
  40.2 1.2 %fusion.6.refs_8_.refs_10_ = bf16[128,2816]{1,0:T(8,128)(2,1)S(1)} fusion(bf16[64,2752]{1,0:T(8,128)(2,1)} %copy-done.5, bf16[64,2752]{1,0:T(8,128)(2,1)} %collective-permute-done.3), kind=kLoop, calls=%fused_computation.11 | loop fusion | flops 2523136 | bytes 1425408 | tf_op jit(solution)/shard_map/concatenate | solution.py:261
  41.3 1.4 %collective-permute-start.8 = (bf16[128,2816]{1,0:T(8,128)(2,1)S(1)}, bf16[128,2816]{1,0:T(8,128)(2,1)}, u32[]{:S(2)}, u32[]{:S(2)}) collective-permute-start(bf16[128,2816]{1,0:T(8,128)(2,1)S(1)} %fusion.6.refs_8_.refs_10_), channel_id=1, source_target_pairs={{0,12},{1,13},{2,14},{3,15},{4,0},{5,1},{6,2},{7,3},{8,4},{9,5},{1... | collective-permute-start | bytes 2162696 | tf_op jit(solution)/shard_map/ppermute | solution.py:253
  42.7 1.4 %collective-permute-start.7 = (bf16[128,2816]{1,0:T(8,128)(2,1)S(1)}, bf16[128,2816]{1,0:T(8,128)(2,1)}, u32[]{:S(2)}, u32[]{:S(2)}) collective-permute-start(bf16[128,2816]{1,0:T(8,128)(2,1)S(1)} %fusion.5.refs_7_.refs_9_), channel_id=1, source_target_pairs={{0,12},{1,13},{2,14},{3,15},{4,0},{5,1},{6,2},{7,3},{8,4},{9,5},{1... | collective-permute-start | bytes 2162696 | tf_op jit(solution)/shard_map/ppermute | solution.py:253
  44.1 0.1 collective-permute-start.6
  44.2 7.7 %all-to-all-done.1 = bf16[16,8,3840]{2,1,0:T(8,128)(2,1)S(1)} async-done(((bf16[16,8,3840]{2,1,0:T(8,128)(2,1)}), bf16[16,8,3840]{2,1,0:T(8,128)(2,1)S(1)}, u32[]{:S(2)}, u32[]{:S(2)}) %all-to-all-start.1) | async-done | bytes 983072 | tf_op jit(solution)/shard_map/all_to_all | solution.py:288
  51.9 0.7 slice.13
  52.6 4.0 %collective-permute-start.1 = (bf16[128,1024]{1,0:T(8,128)(2,1)}, bf16[128,1024]{1,0:T(8,128)(2,1)}, u32[]{:S(2)}, u32[]{:S(2)}) collective-permute-start(bf16[128,1024]{1,0:T(8,128)(2,1)} %slice.13), channel_id=1, source_target_pairs={{0,64},{64,0},{128,192},{192,128},{1,65},{65,1},{129,193},{193,129... | collective-permute-start | bytes 786440 | tf_op jit(solution)/shard_map/ppermute | solution.py:291
  57.3 0.0 copy-start.3
  57.3 0.1 pad_add_fusion.refs_0_.refs_2_
  57.4 0.0 copy-done.1
  57.4 0.8 shard_map.92.refs_5_.refs_7_
  58.2 0.5 copy-done.3
  58.7 0.1 pad.16.refs_6_.refs_8_
  58.8 0.0 copy-start.2
  58.8 0.5 collective-permute-done.5.refs_9_.refs_11_
  59.2 0.0 collective-permute-start.9
  59.2 0.0 collective-permute-done.8.refs_12_.refs_14_
  59.3 2.7 %collective-permute-start.10 = (bf16[128,2816]{1,0:T(8,128)(2,1)}, bf16[128,2816]{1,0:T(8,128)(2,1)S(1)}, u32[]{:S(2)}, u32[]{:S(2)}) collective-permute-start(bf16[128,2816]{1,0:T(8,128)(2,1)} %collective-permute-done.8.refs_12_.refs_14_), channel_id=1, source_target_pairs={{0,12},{1,13},{2,14},{3,15},{4,0},{5,1},{6,2},{7,3},{8,4},{9,5},{1... | collective-permute-start | bytes 2162696 | tf_op jit(solution)/shard_map/ppermute | solution.py:253
  62.0 0.0 collective-permute-done.1.refs_2_
  62.0 1.9 %collective-permute-start = (bf16[128,2816]{1,0:T(8,128)(2,1)S(1)}, bf16[128,2816]{1,0:T(8,128)(2,1)S(1)}, u32[]{:S(2)}, u32[]{:S(2)}) collective-permute-start(bf16[128,2816]{1,0:T(8,128)(2,1)S(1)} %slice.12), channel_id=1, source_target_pairs={{0,16},{16,0},{32,48},{48,32},{1,17},{17,1},{33,49},{49,33},{2,18}... | collective-permute-start | bytes 2162696 | tf_op jit(solution)/shard_map/ppermute | solution.py:290
  63.9 1.8 %shard_map.91.refs_4_.refs_6_ = bf16[1024,256]{1,0:T(8,128)(2,1)S(1)} custom-call(s32[4]{0:T(128)S(1)} %pad_add_fusion.refs_0_.refs_2_, bf16[128,3840]{1,0:T(8,128)(2,1)S(1)} %bitcast.18, bf16[128,1024]{1,0:T(8,128)(2,1)} %collective-permute-done.1.refs_2_), custom_call_target="tpu_custom_call" | custom-call | bytes 1048576 | tf_op jit(solution)/shard_map/pallas_call | solution.py:44
  65.7 0.1 collective-permute-done.7.refs_11_.refs_13_
  65.8 1.2 %collective-permute-done.6.refs_10_.refs_12_ = bf16[128,2816]{1,0:T(8,128)(2,1)} collective-permute-done((bf16[128,2816]{1,0:T(8,128)(2,1)S(1)}, bf16[128,2816]{1,0:T(8,128)(2,1)}, u32[]{:S(2)}, u32[]{:S(2)}) %collective-permute-start.6) | collective-permute-done | bytes 720928 | tf_op jit(solution)/shard_map/ppermute | solution.py:253
  67.0 0.0 copy-done.2
  67.0 4.0 %shard_map.93.refs_5_ = f32[8,256]{1,0:T(8,128)S(1)} custom-call(s32[2,4]{1,0:T(2,128)S(1)} %bitcast.23, s32[1]{0:T(128)S(6)} %copy.14.refs_1_, s32[4]{0:T(128)S(1)} %pad_add_fusion.refs_0_.refs_2_, bf16[128,3840]{1,0:T(8,128)(2,1)S(1)} %bitcast.19, bf16[1024,256]{1,0:T(8,128)(2,1)S(1)} %shard_map.91.refs_4_.refs_6_, ...), custom_call_target="tpu_custom_call" | custom-call | flops 8858370048 | bytes 12845056 | tf_op jit(solution)/shard_map/pallas_call | solution.py:214
  70.9 3.7 %collective-permute-done.9.refs_15_ = bf16[128,2816]{1,0:T(8,128)(2,1)S(1)} collective-permute-done((bf16[128,2816]{1,0:T(8,128)(2,1)}, bf16[128,2816]{1,0:T(8,128)(2,1)S(1)}, u32[]{:S(2)}, u32[]{:S(2)}) %collective-permute-start.9) | collective-permute-done | bytes 720928 | tf_op jit(solution)/shard_map/ppermute | solution.py:253
  74.6 0.0 collective-permute-done.10.refs_16_
  74.6 4.3 %collective-permute-done.refs_4_ = bf16[128,2816]{1,0:T(8,128)(2,1)S(1)} collective-permute-done((bf16[128,2816]{1,0:T(8,128)(2,1)S(1)}, bf16[128,2816]{1,0:T(8,128)(2,1)S(1)}, u32[]{:S(2)}, u32[]{:S(2)}) %collective-permute-start) | collective-permute-done | bytes 720928 | tf_op jit(solution)/shard_map/ppermute | solution.py:290
  78.9 15.7 %shard_map.94 = f32[8,128]{1,0:T(8,128)S(1)} custom-call(s32[2,4]{1,0:T(2,128)S(1)} %bitcast.24, s32[1]{0:T(128)S(6)} %copy.14.refs_1_, s32[4]{0:T(128)S(1)} %pad_add_fusion.refs_0_.refs_2_, bf16[128,3840]{1,0:T(8,128)(2,1)S(1)} %bitcast.20, bf16[128,2816]{1,0:T(8,128)(2,1)S(1)} %collective-permute-done.refs_4_, f32[8,256]{1,0:T(8,128)S(1)} %shard_map.93.refs_5_, ...), custom_call_target="tpu_custom_call" | custom-call | flops 11811160064 | bytes 15728640 | tf_op jit(solution)/shard_map/pallas_call | solution.py:214
  94.6 17.7 %all_to_all.15 = f32[16,8,128]{2,1,0:T(8,128)S(1)} all-to-all(f32[16,8,128]{2,1,0:T(8,128)S(1)} %broadcast_in_dim.5), channel_id=1, replica_groups=mesh['layer'=4,'query'=4,'doc'=16] {'layer','query'}, dimensions={0} | all-to-all | bytes 131072 | tf_op jit(solution)/shard_map/all_to_all | solution.py:303
  112.4 0.7 reshape.23
  (4 shorter events, 0.1 us)
Async XLA Ops:
  0.0 3.1 %copy-start = (bf16[256,1024]{1,0:T(8,128)(2,1)S(1)}, bf16[256,1024]{1,0:T(8,128)(2,1)}, u32[]{:S(2)}) copy-start(bf16[256,1024]{1,0:T(8,128)(2,1)} %param.12) | copy-start | bytes 1572868
  3.0 0.9 copy-start.6
  5.3 7.7 %copy-start.4 = (bf16[2752,64]{0,1:T(8,128)(2,1)S(1)}, bf16[2752,64]{0,1:T(8,128)(2,1)}, u32[]{:S(2)}) copy-start(bf16[2752,64]{0,1:T(8,128)(2,1)} %param.13) | copy-start | bytes 1056772
  5.3 23.2 %all-to-all-start = ((f16[16,8,3840]{2,1,0:T(8,128)(2,1)}), f16[16,8,3840]{2,1,0:T(8,128)(2,1)S(1)}, u32[]{:S(2)}, u32[]{:S(2)}) async-start(f16[16,8,3840]{2,1,0:T(8,128)(2,1)} %fusion), calls=%async_computation | async-start | bytes 1966080 | tf_op jit(solution)/shard_map/all_to_all | solution.py:278
  13.0 26.4 %collective-permute-start.4 = (bf16[64,2752]{1,0:T(8,128)(2,1)S(1)}, bf16[64,2752]{1,0:T(8,128)(2,1)S(1)}, u32[]{:S(2)}, u32[]{:S(2)}) collective-permute-start(bf16[64,2752]{1,0:T(8,128)(2,1)S(1)} %bitcast.26), channel_id=1, source_target_pairs={{0,2},{1,3},{2,0},{3,1},{4,6},{5,7},{6,4},{7,5},{8,10},{9,11},{10,... | collective-permute-start | bytes 1056776 | tf_op jit(solution)/shard_map/ppermute | solution.py:253
  16.0 24.2 %collective-permute-start.3 = (bf16[64,2752]{1,0:T(8,128)(2,1)S(1)}, bf16[64,2752]{1,0:T(8,128)(2,1)}, u32[]{:S(2)}, u32[]{:S(2)}) collective-permute-start(bf16[64,2752]{1,0:T(8,128)(2,1)S(1)} %bitcast.27), channel_id=1, source_target_pairs={{0,3},{1,0},{2,1},{3,2},{4,7},{5,4},{6,5},{7,6},{8,11},{9,8},{10,9... | collective-permute-start | bytes 1056776 | tf_op jit(solution)/shard_map/ppermute | solution.py:253
  16.9 20.0 %collective-permute-start.2 = (bf16[64,2752]{1,0:T(8,128)(2,1)S(1)}, bf16[64,2752]{1,0:T(8,128)(2,1)}, u32[]{:S(2)}, u32[]{:S(2)}) collective-permute-start(bf16[64,2752]{1,0:T(8,128)(2,1)S(1)} %bitcast.28), channel_id=1, source_target_pairs={{0,1},{1,2},{2,3},{3,0},{4,5},{5,6},{6,7},{7,4},{8,9},{9,10},{10,1... | collective-permute-start | bytes 1056776 | tf_op jit(solution)/shard_map/ppermute | solution.py:253
  29.7 22.3 %all-to-all-start.1 = ((bf16[16,8,3840]{2,1,0:T(8,128)(2,1)}), bf16[16,8,3840]{2,1,0:T(8,128)(2,1)S(1)}, u32[]{:S(2)}, u32[]{:S(2)}) async-start(bf16[16,8,3840]{2,1,0:T(8,128)(2,1)} %broadcast_in_dim.4), calls=%async_computation.1 | async-start | bytes 1966080 | tf_op jit(solution)/shard_map/all_to_all | solution.py:288
  36.9 20.5 %copy-start.1 = (bf16[4,64,1024]{2,1,0:T(8,128)(2,1)S(1)}, bf16[4,64,1024]{2,1,0:T(8,128)(2,1)}, u32[]{:S(2)}) copy-start(bf16[4,64,1024]{2,1,0:T(8,128)(2,1)} %param.15) | copy-start | bytes 1572868
  38.0 21.3 %collective-permute-start.5 = (bf16[128,2816]{1,0:T(8,128)(2,1)S(1)}, bf16[128,2816]{1,0:T(8,128)(2,1)}, u32[]{:S(2)}, u32[]{:S(2)}) collective-permute-start(bf16[128,2816]{1,0:T(8,128)(2,1)S(1)} %fusion.5.refs_7_.refs_9_), channel_id=1, source_target_pairs={{0,4},{1,5},{2,6},{3,7},{4,8},{5,9},{6,10},{7,11},{8,12},{9,13},{1... | collective-permute-start | bytes 2162696 | tf_op jit(solution)/shard_map/ppermute | solution.py:253
  39.4 0.7 copy-start.5
  41.3 17.9 %collective-permute-start.8 = (bf16[128,2816]{1,0:T(8,128)(2,1)S(1)}, bf16[128,2816]{1,0:T(8,128)(2,1)}, u32[]{:S(2)}, u32[]{:S(2)}) collective-permute-start(bf16[128,2816]{1,0:T(8,128)(2,1)S(1)} %fusion.6.refs_8_.refs_10_), channel_id=1, source_target_pairs={{0,12},{1,13},{2,14},{3,15},{4,0},{5,1},{6,2},{7,3},{8,4},{9,5},{1... | collective-permute-start | bytes 2162696 | tf_op jit(solution)/shard_map/ppermute | solution.py:253
  42.7 23.1 %collective-permute-start.7 = (bf16[128,2816]{1,0:T(8,128)(2,1)S(1)}, bf16[128,2816]{1,0:T(8,128)(2,1)}, u32[]{:S(2)}, u32[]{:S(2)}) collective-permute-start(bf16[128,2816]{1,0:T(8,128)(2,1)S(1)} %fusion.5.refs_7_.refs_9_), channel_id=1, source_target_pairs={{0,12},{1,13},{2,14},{3,15},{4,0},{5,1},{6,2},{7,3},{8,4},{9,5},{1... | collective-permute-start | bytes 2162696 | tf_op jit(solution)/shard_map/ppermute | solution.py:253
  44.1 22.9 %collective-permute-start.6 = (bf16[128,2816]{1,0:T(8,128)(2,1)S(1)}, bf16[128,2816]{1,0:T(8,128)(2,1)}, u32[]{:S(2)}, u32[]{:S(2)}) collective-permute-start(bf16[128,2816]{1,0:T(8,128)(2,1)S(1)} %fusion.6.refs_8_.refs_10_), channel_id=1, source_target_pairs={{0,4},{1,5},{2,6},{3,7},{4,8},{5,9},{6,10},{7,11},{8,12},{9,13},{1... | collective-permute-start | bytes 2162696 | tf_op jit(solution)/shard_map/ppermute | solution.py:253
  52.6 9.3 %collective-permute-start.1 = (bf16[128,1024]{1,0:T(8,128)(2,1)}, bf16[128,1024]{1,0:T(8,128)(2,1)}, u32[]{:S(2)}, u32[]{:S(2)}) collective-permute-start(bf16[128,1024]{1,0:T(8,128)(2,1)} %slice.13), channel_id=1, source_target_pairs={{0,64},{64,0},{128,192},{192,128},{1,65},{65,1},{129,193},{193,129... | collective-permute-start | bytes 786440 | tf_op jit(solution)/shard_map/ppermute | solution.py:291
  57.3 1.4 %copy-start.3 = (bf16[4,64,2752]{2,1,0:T(8,128)(2,1)S(1)}, bf16[4,64,2752]{2,1,0:T(8,128)(2,1)}, u32[]{:S(2)}) copy-start(bf16[4,64,2752]{2,1,0:T(8,128)(2,1)} %param.14) | copy-start | bytes 4227076
  58.8 8.2 %copy-start.2 = (s32[4,2]{0,1:T(2,128)S(1)}, s32[4,2]{0,1:T(2,128)}, u32[]{:S(2)}) copy-start(s32[4,2]{0,1:T(2,128)} %param.16) | copy-start | bytes 100
  59.2 15.3 %collective-permute-start.9 = (bf16[128,2816]{1,0:T(8,128)(2,1)}, bf16[128,2816]{1,0:T(8,128)(2,1)S(1)}, u32[]{:S(2)}, u32[]{:S(2)}) collective-permute-start(bf16[128,2816]{1,0:T(8,128)(2,1)} %collective-permute-done.5.refs_9_.refs_11_), channel_id=1, source_target_pairs={{0,4},{1,5},{2,6},{3,7},{4,8},{5,9},{6,10},{7,11},{8,12},{9,13},{1... | collective-permute-start | bytes 2162696 | tf_op jit(solution)/shard_map/ppermute | solution.py:253
  59.3 15.3 %collective-permute-start.10 = (bf16[128,2816]{1,0:T(8,128)(2,1)}, bf16[128,2816]{1,0:T(8,128)(2,1)S(1)}, u32[]{:S(2)}, u32[]{:S(2)}) collective-permute-start(bf16[128,2816]{1,0:T(8,128)(2,1)} %collective-permute-done.8.refs_12_.refs_14_), channel_id=1, source_target_pairs={{0,12},{1,13},{2,14},{3,15},{4,0},{5,1},{6,2},{7,3},{8,4},{9,5},{1... | collective-permute-start | bytes 2162696 | tf_op jit(solution)/shard_map/ppermute | solution.py:253
  62.0 16.9 %collective-permute-start = (bf16[128,2816]{1,0:T(8,128)(2,1)S(1)}, bf16[128,2816]{1,0:T(8,128)(2,1)S(1)}, u32[]{:S(2)}, u32[]{:S(2)}) collective-permute-start(bf16[128,2816]{1,0:T(8,128)(2,1)S(1)} %slice.12), channel_id=1, source_target_pairs={{0,16},{16,0},{32,48},{48,32},{1,17},{17,1},{33,49},{49,33},{2,18}... | collective-permute-start | bytes 2162696 | tf_op jit(solution)/shard_map/ppermute | solution.py:290
